TPU v7x, 256 devices: a whole 4x4x8 slice. The times are simulated.
256 devices in a mesh: pr: 8 (over z), pc: 8 (over x, core), gz: 4 (over y).
Axes of the slice: x: 4, y: 4, z: 8, core: 2. Of those that a mesh axis runs over, the one named last changes fastest.
Arguments:
- rhs_leaf: bfloat16 [4, 512, 128, 256], P('gz', ('pr', 'pc')), may hold values from -16 to 16
- rhs_mid: bfloat16 [4, 256, 256, 256], P('gz', ('pr', 'pc')), may hold values from -6 to 6
- rhs_top: bfloat16 [64, 512, 256], P('pr', 'pc'), may hold values from -6 to 6
- inv_leaf: bfloat16 [4, 512, 128, 128], P('gz', ('pr', 'pc')), may hold values from -1 to 1.5, as said below
- inv_mid: bfloat16 [4, 256, 256, 256], P('gz', ('pr', 'pc')), may hold values from -1 to 1.5, as said below
- inv_top: bfloat16 [64, 512, 512], P('pr', 'pc'), may hold values from -1 to 1.5, as said below
- off_leaf_mid: bfloat16 [4, 512, 256, 128], P('gz', ('pr', 'pc')), may hold values from -0.375 to 0.375
- off_leaf_top: bfloat16 [4, 512, 512, 128], P('gz', ('pr', 'pc')), may hold values from -0.25 to 0.25
- off_leaf_out: bfloat16 [4, 512, 1024, 128], P('gz', ('pr', 'pc')), may hold values from -0.0234375 to 0.0234375
- off_mid_top: bfloat16 [4, 256, 512, 256], P('gz', ('pr', 'pc')), may hold values from -0.1875 to 0.1875
- off_mid_out: bfloat16 [4, 256, 1024, 256], P('gz', ('pr', 'pc')), may hold values from -0.0234375 to 0.0234375
- off_top_out: bfloat16 [64, 1024, 512], P('pr', 'pc'), may hold values from -0.0625 to 0.0625
- parent_leaf: int32 [4, 512, 1], P('gz', ('pr', 'pc')), may hold values from 0 to 255, as said below
- parent_mid: int32 [4, 256, 1], P('gz', ('pr', 'pc')), may hold values from 0 to 63, as said below
- width_leaf: int32 [4, 512], P('gz', ('pr', 'pc')), may hold values from 1 to 128, 49152 in all within a row
- width_mid: int32 [4, 256], P('gz', ('pr', 'pc')), may hold values from 1 to 256, 49152 in all within a row
- width_top: int32 [64], P('pr'), may hold values from 1 to 512, 24576 in all
- pattern_leaf: int32 [4, 512, 2], P('gz', ('pr', 'pc')), may hold values 0 or 1
- pattern_mid: int32 [4, 256], P('gz', ('pr', 'pc')), may hold values 0 or 1
Outputs:
- leaf_solution: bfloat16 [4, 512, 128, 256], P('gz', ('pr', 'pc'))
- mid_solution: bfloat16 [4, 256, 256, 256], P('gz', ('pr', 'pc'))
- top_solution: bfloat16 [64, 512, 256], P(('pr', 'gz'), 'pc')
- outer_update: float32 [1024, 256], P('pc', ('pr', 'gz'))
Inputs may be any that keep to these rules, and one draw needn't show every extreme that they name: `inv_leaf`: each 128 x 128 block is lower triangular with its diagonal between 0.5 and 1.5. `inv_mid`: each 256 x 256 block is lower triangular with its diagonal between 0.5 and 1.5. `inv_top`: each 512 x 512 block is lower triangular with its diagonal between 0.5 and 1.5. `parent_leaf`: the leaves in each aligned block of 8 (per layer) have their parents among the matching aligned block of 4 level-one supernodes, and each of those has exactly two of them as children. `parent_mid`: Level-one supernodes are taken in aligned blocks of 32 per layer, the i-th block lying under process row i; each one's parent is among the 8 level-two supernodes of that process row.
All inputs are finite; a program needn't handle non-finite values. No bound on the sum of `width_leaf` or of `width_mid` or of `width_top` or of `pattern_leaf` or of `pattern_mid` on one device may be relied on, other than what follows from the above.
Results may differ from a plain program's by a relative error of at most 0.0062.
Values may be sent and summed in bfloat16 or wider, within the bound.
A program may use at most 64 MiB of HBM per device.

v0:
```python
import jax
import jax.numpy as jnp
from jax import lax
from jax.sharding import PartitionSpec as P


def solve_local(inverse, right_side, widths):
    matrix_product = jnp.einsum(
        "kpw,kwr->kpr", inverse, right_side, preferred_element_type=jnp.float32
    )
    row_ids = jnp.arange(inverse.shape[1], dtype=jnp.int32)
    active_mask = row_ids[None, :, None] < widths[:, None, None]
    return jnp.where(active_mask, matrix_product, jnp.float32(0.0)).astype(jnp.bfloat16)


def masked_rows(values, widths, offset):
    row_ids = offset + jnp.arange(values.shape[1], dtype=jnp.int32)
    active_mask = row_ids[None, :] < widths[:, None]
    return jnp.where(active_mask[:, :, None], values, jnp.float32(0.0))


def fold_step(matrix, incoming):
    return jnp.einsum("qmw,qwr->qmr", matrix, incoming, preferred_element_type=jnp.float32)


def on_device(
    rhs_leaf,
    rhs_mid,
    rhs_top,
    inv_leaf,
    inv_mid,
    inv_top,
    off_leaf_mid,
    off_leaf_top,
    off_leaf_out,
    off_mid_top,
    off_mid_out,
    off_top_out,
    parent_leaf,
    parent_mid,
    width_leaf,
    width_mid,
    width_top,
    pattern_leaf,
    pattern_mid,
):
    col_index = lax.axis_index("pc")
    row_index = lax.axis_index("pr")
    layer_index = lax.axis_index("gz")
    columns = lax.axis_size("pc")
    layers = lax.axis_size("gz")
    num_rhs = rhs_leaf.shape[3]
    mid_count = rhs_mid.shape[1]
    top_count = rhs_top.shape[0]
    top_slab = rhs_top.shape[1]
    layer_share = top_count // layers
    share_start = layer_index * layer_share
    device_index = row_index * columns + col_index
    leaf_x = solve_local(inv_leaf[0], rhs_leaf[0], width_leaf[0])
    leaf_parent = parent_leaf[0, :, 0] - device_index * mid_count
    to_mid = (jnp.arange(mid_count, dtype=jnp.int32)[:, None] == leaf_parent[None, :]).astype(
        jnp.float32
    )
    leaf_mid = jnp.einsum(
        "qmw,qwr->qmr", off_leaf_mid[0], leaf_x, preferred_element_type=jnp.float32
    )
    mid_sums = jnp.einsum("jq,qmr->jmr", to_mid, leaf_mid, precision=lax.Precision.HIGHEST)
    mid_input = (rhs_mid[0].astype(jnp.float32) - mid_sums).astype(jnp.bfloat16)
    mid_x = solve_local(inv_mid[0], mid_input, width_mid[0])
    mid_top = parent_mid[0, :, 0] - row_index * top_count
    middle_toward_apex = (
        jnp.arange(top_count, dtype=jnp.int32)[:, None] == mid_top[None, :]
    ).astype(jnp.float32)
    leaf_toward_apex = (
        jnp.dot(middle_toward_apex, to_mid, precision=lax.Precision.HIGHEST)
        * pattern_leaf[0, :, 0].astype(jnp.float32)[None, :]
    )
    leaf_block = off_leaf_top[0]
    mid_block = off_mid_top[0]
    leaf_contribution = jnp.einsum(
        "qmw,qwr->qmr", leaf_block, leaf_x, preferred_element_type=jnp.float32
    )
    middle_contribution = jnp.einsum(
        "qmw,qwr->qmr", mid_block, mid_x, preferred_element_type=jnp.float32
    )
    group_collected = jnp.einsum(
        "yt,tpn->pyn", leaf_toward_apex, leaf_contribution, precision=lax.Precision.HIGHEST
    )
    whole_term = group_collected + jnp.einsum(
        "yt,tpn->pyn", middle_toward_apex, middle_contribution, precision=lax.Precision.HIGHEST
    )
    arranged = whole_term.reshape(columns, top_slab, layers, layer_share, num_rhs)
    arranged = jnp.transpose(arranged, (0, 2, 1, 3, 4)).reshape(
        columns * layers * top_slab, layer_share, num_rhs
    )
    share_sums = lax.psum_scatter(arranged, ("pc", "gz"), scatter_dimension=0, tiled=True)
    top_sums = jnp.transpose(share_sums, (1, 0, 2))
    top_rhs = lax.dynamic_slice_in_dim(rhs_top, share_start, layer_share, 0)
    top_inv = lax.dynamic_slice_in_dim(inv_top, share_start, layer_share, 0)
    top_widths = lax.dynamic_slice_in_dim(width_top, share_start, layer_share, 0)
    top_input = (top_rhs.astype(jnp.float32) - top_sums).astype(jnp.bfloat16)
    top_solved = fold_step(top_inv, lax.all_gather(top_input, "pc", axis=1, tiled=True))
    top_piece = masked_rows(top_solved, top_widths, col_index * top_slab).astype(jnp.bfloat16)
    top_outer_block = lax.dynamic_slice_in_dim(off_top_out, share_start, layer_share, 0)
    outer_slab = off_top_out.shape[1]
    top_terms = fold_step(top_outer_block, lax.all_gather(top_piece, "pc", axis=1, tiled=True))
    leaf_flagged = leaf_x * pattern_leaf[0, :, 1].astype(jnp.bfloat16)[:, None, None]
    mid_flagged = mid_x * pattern_mid[0].astype(jnp.bfloat16)[:, None, None]
    outer_local = jnp.einsum(
        "qmw,qwr->mr", off_leaf_out[0], leaf_flagged, preferred_element_type=jnp.float32
    )
    outer_local = outer_local + jnp.einsum(
        "qmw,qwr->mr", off_mid_out[0], mid_flagged, preferred_element_type=jnp.float32
    )
    own_rows = lax.dynamic_slice_in_dim(outer_local, col_index * outer_slab, outer_slab, 0)
    outer_local = lax.dynamic_update_slice_in_dim(
        outer_local, own_rows + jnp.sum(top_terms, axis=0), col_index * outer_slab, 0
    )
    outer_rows = lax.psum_scatter(outer_local, "pc", scatter_dimension=0, tiled=True)
    outer_part = lax.psum_scatter(outer_rows, ("pr", "gz"), scatter_dimension=1, tiled=True)
    return (leaf_x[None], mid_x[None], top_piece, outer_part)


def solution(mesh):
    return jax.shard_map(
        on_device,
        mesh=mesh,
        in_specs=(
            P("gz", ("pr", "pc"), None, None),
            P("gz", ("pr", "pc"), None, None),
            P("pr", "pc", None),
            P("gz", ("pr", "pc"), None, None),
            P("gz", ("pr", "pc"), None, None),
            P("pr", "pc", None),
            P("gz", ("pr", "pc"), None, None),
            P("gz", ("pr", "pc"), None, None),
            P("gz", ("pr", "pc"), None, None),
            P("gz", ("pr", "pc"), None, None),
            P("gz", ("pr", "pc"), None, None),
            P("pr", "pc", None),
            P("gz", ("pr", "pc"), None),
            P("gz", ("pr", "pc"), None),
            P("gz", ("pr", "pc")),
            P("gz", ("pr", "pc")),
            P("pr"),
            P("gz", ("pr", "pc"), None),
            P("gz", ("pr", "pc")),
        ),
        out_specs=(
            P("gz", ("pr", "pc"), None, None),
            P("gz", ("pr", "pc"), None, None),
            P(("pr", "gz"), "pc", None),
            P("pc", ("pr", "gz")),
        ),
        check_vma=False,
    )
```

profile of v0, /device:TPU:1, one launch (start us, length us, event | category | flops | bytes accessed | tf_op | source)
XLA Modules:
  0.0 361.1 jit_solution(1286182512522235817)
XLA Ops:
  8.8 1.4 fusion.17
  10.2 4.1 %fusion.25 = f32[8,256,512]{2,1,0:T(8,128)} fusion(bf16[8,128,256]{2,1,0:T(8,128)(2,1)S(1)} %fusion.17, bf16[1,8,512,128]{3,2,1,0:T(8,128)(2,1)} %param.26), kind=kOutput, calls=%fused_computation.27 | convolution fusion | flops 268435456 | bytes 5767168 | tf_op jit(solution)/shard_map/qmw,qwr->qmr/dot_general | solution.py:80
  14.3 5.5 %copy.36 = f32[8,256,512]{1,0,2:T(8,128)} copy(f32[8,256,512]{2,1,0:T(8,128)} %fusion.25) | data formatting | bytes 8388608 | tf_op jit(solution)/shard_map/qmw,qwr->qmr/dot_general | solution.py:80
  19.8 1.8 convolution_bitcast_fusion
  21.7 3.1 copy.33
  24.9 2.7 fusion.41
  27.6 1.7 fusion.16
  29.3 1.8 fusion.23
  31.1 2.9 copy.37
  34.3 5.6 %fusion = f32[512,256,8]{1,2,0:T(8,128)S(1)} fusion(f32[8,8,1]{1,0,2:T(8,128)S(1)} %fusion.21, f32[8,256,512]{1,0,2:T(8,128)} %copy.36), kind=kOutput, calls=%fused_computation | convolution fusion | flops 100663296 | bytes 8388864 | tf_op jit(solution)/shard_map/yt,tpn->pyn/dot_general | solution.py:86
  39.9 4.4 %add_bitcast_fusion = f32[512,8,256]{2,1,0:T(8,128)} fusion(f32[512,256,8]{1,2,0:T(8,128)S(1)} %fusion, f32[4,256,512]{1,0,2:T(4,128)S(1)} %copy-done.1, s32[4]{0:T(128)S(1)} %subtract_bitcast_fusion), kind=kOutput, calls=%fused_computation.2 | convolution fusion | flops 51380256 | bytes 10485776 | tf_op jit(solution)/shard_map/yt,tpn->pyn/dot_general | solution.py:89
  44.3 5.9 %reshape.136 = f32[8,64,4,2,256]{4,3,2,1,0:T(2,128)} reshape(f32[512,8,256]{2,1,0:T(8,128)} %add_bitcast_fusion) | data formatting | bytes 8388608 | tf_op jit(solution)/shard_map/reshape | solution.py:92
  50.2 5.5 %copy.29 = f32[8,4,64,2,256]{4,2,1,0,3:T(8,128)} copy(f32[8,4,64,2,256]{4,3,1,2,0:T(2,128)} %bitcast.102) | data formatting | bytes 8388608 | tf_op jit(solution)/shard_map/transpose | solution.py:93
  58.3 1.0 copy-done.3
  59.3 1.0 copy.43
  60.4 87.1 %reduce-scatter.3.cloned.1.call-done = f32[64,2,256]{2,0,1:T(8,128)} async-done(((f32[2048,2,256]{2,0,1:T(8,128)}), f32[64,2,256]{2,0,1:T(8,128)}) %reduce-scatter.3.cloned.1.call-update) | async-done | bytes 131088 | tf_op jit(solution)/shard_map/reduce_scatter | solution.py:96
  148.4 15.2 %all_gather.6 = bf16[2,512,256]{2,1,0:T(8,128)(2,1)S(1)} all-gather(bf16[2,64,256]{2,1,0:T(8,128)(2,1)S(1)} %fusion.37), channel_id=1, replica_groups=mesh['pr'=8,'pc'=8,'gz'=4] {'pc'}, dimensions={1}, use_global_device_ids=true | all-gather | bytes 589824 | tf_op jit(solution)/shard_map/all_gather | solution.py:102
  163.7 1.1 fusion.20
  164.8 13.2 %all_gather.7 = bf16[2,512,256]{2,1,0:T(8,128)(2,1)S(1)} all-gather(bf16[2,64,256]{2,1,0:T(8,128)(2,1)S(1)} %fusion.20), channel_id=1, replica_groups=mesh['pr'=8,'pc'=8,'gz'=4] {'pc'}, dimensions={1}, use_global_device_ids=true | all-gather | bytes 589824 | tf_op jit(solution)/shard_map/all_gather | solution.py:106
  178.1 2.0 fusion.19
  180.1 31.0 %reduce-scatter.5.cloned.1.call-done = f32[128,256]{0,1:T(8,128)} async-done(((f32[1024,256]{0,1:T(8,128)}), f32[128,256]{0,1:T(8,128)}) %reduce-scatter.5.cloned.1.call-update) | async-done | bytes 131088 | tf_op jit(solution)/shard_map/reduce_scatter | solution.py:119
  211.1 1.0 copy.32
  213.4 139.9 %all-reduce.3.cloned.1.call-done = f32[128,256]{0,1:T(8,128)} async-done(((f32[128,256]{0,1:T(8,128)}), f32[128,256]{0,1:T(8,128)}) %all-reduce.3.cloned.1.call-update) | async-done | bytes 131088
  353.3 1.3 constant_dynamic-slice_fusion
  (48 shorter events, 6.2 us)
Async XLA Ops:
  7.2 49.2 %copy-start = (bf16[1,8,1024,128]{3,2,1,0:T(8,128)(2,1)S(1)}, bf16[1,8,1024,128]{3,2,1,0:T(8,128)(2,1)}, u32[]{:S(2)}) copy-start(bf16[1,8,1024,128]{3,2,1,0:T(8,128)(2,1)} %param.27) | copy-start | bytes 6291460
  7.2 140.3 %reduce-scatter.3.cloned.1.call-start = ((), (), s32[]{:S(2)}) async-start(), calls=%async_computation.2 | async-start | bytes 4325376 | tf_op jit(solution)/shard_map/reduce_scatter | solution.py:96
  10.2 46.2 %copy-start.2 = (bf16[8,128,256]{2,1,0:T(8,128)(2,1)}, bf16[8,128,256]{2,1,0:T(8,128)(2,1)S(1)}, u32[]{:S(2)}) copy-start(bf16[8,128,256]{2,1,0:T(8,128)(2,1)S(1)} %fusion.17) | copy-start | bytes 1572868
  14.3 5.5 %copy-start.6 = (bf16[1,8,256,128]{3,2,1,0:T(8,128)(2,1)S(1)}, bf16[1,8,256,128]{3,2,1,0:T(8,128)(2,1)}, u32[]{:S(2)}) copy-start(bf16[1,8,256,128]{3,2,1,0:T(8,128)(2,1)} %param.25) | copy-start | bytes 1572868
  21.7 3.1 copy-start.10
  21.7 3.2 copy-start.8
  21.7 3.2 copy-start.9
  27.6 1.7 copy-start.5
  34.3 5.6 %copy-start.1 = (f32[4,256,512]{1,0,2:T(4,128)S(1)}, f32[4,256,512]{1,0,2:T(4,128)}, u32[]{:S(2)}) copy-start(f32[4,256,512]{1,0,2:T(4,128)} %copy.37) | copy-start | bytes 6291460
  55.7 0.7 copy-start.11
  55.7 155.4 %reduce-scatter.5.cloned.1.call-start = ((), (), s32[]{:S(2)}) async-start(), calls=%async_computation.3 | async-start | bytes 1179648 | tf_op jit(solution)/shard_map/reduce_scatter | solution.py:119
  55.9 1.6 copy-start.4
  58.3 1.0 copy-start.3
  58.3 2.0 copy-start.12
  164.8 189.8 %copy-start.7 = (bf16[2,64,256]{2,1,0:T(8,128)(2,1)}, bf16[2,64,256]{2,1,0:T(8,128)(2,1)S(1)}, u32[]{:S(2)}) copy-start(bf16[2,64,256]{2,1,0:T(8,128)(2,1)S(1)} %fusion.20) | copy-start | bytes 196612
  164.8 47.3 %copy-start.13 = (u32[256]{0:T(256)S(1)}, u32[256]{0:T(256)}, u32[]{:S(2)}) copy-start(u32[256]{0:T(256)} %constant.46) | copy-start | bytes 3076
  180.1 173.2 %all-reduce.3.cloned.1.call-start = ((), (), s32[]{:S(2)}) async-start(), calls=%async_computation.4 | async-start | bytes 262144
Sparse Core Ops, SparseCore 0:
  55.8 91.6 reduce-scatter.2
  180.2 30.8 reduce-scatter.4
  215.0 138.2 all-reduce.2
where the time goes:
time: 365 us; the launch traced here: 361 us
  waiting for transfers between devices  258 us (71%)
  matrix products  28.6 us (8%)
  local copies, waits for them, and re-layouts  28.5 us (8%)
  blocking collectives  28.5 us (8%)
  between operations  14.6 us (4%)
    unnamed x4, waiting for transfers between devices  140 us
    reduce_scatter x1, waiting for transfers between devices, on_device(): lax.psum_scatter(arranged, ('pc', 'gz'), scatter_dimension=0, tiled=True)  87.1 us
    reduce_scatter x1, waiting for transfers between devices, on_device(): lax.psum_scatter(outer_local, 'pc', scatter_dimension=0, tiled=True)  31 us
    all_gather x1, blocking collectives, on_device(): lax.all_gather(top_input, 'pc', axis=1, tiled=True)  15.2 us
    all_gather x1, blocking collectives, on_device(): lax.all_gather(top_piece, 'pc', axis=1, tiled=True)  13.2 us
  transfers between devices with their start and end apart: 3, of which 3 were waited for; matrix products, arithmetic and copies ran while one was open for 1% of the time, Pallas kernels for 0%

commit v1 on v0

v1 whole, which is shorter than its diff:
```python
import functools

import jax
import jax.numpy as jnp
from jax import lax
from jax.experimental import pallas as pl
from jax.experimental.pallas import tpu as pltpu
from jax.sharding import PartitionSpec as P

MESH_IDS = pl.DeviceIdType.MESH
F32 = jnp.float32
BF16 = jnp.bfloat16
LANES = 128


def dot(a, b):
    return jnp.dot(a, b, preferred_element_type=F32)


def live_rows(values, first_row, width):
    row_ids = first_row + lax.broadcasted_iota(jnp.int32, values.shape, 0)
    return jnp.where(row_ids < width, values, 0.0)


def flagged(values, flag):
    return jnp.where(flag != 0, values, jnp.zeros_like(values))


def subtree_kernel(
    parent_leaf, parent_mid, width_leaf, width_mid, pattern_leaf,
    rhs_leaf, inv_leaf, off_leaf_mid, rhs_mid, inv_mid, off_leaf_top, off_mid_top,
    leaf_out, mid_out, top_out,
    rl, il, lm, rm, im, lt, mt, xl, xm, top, load_sems, store_sems,
):
    leaves, mids, tops = xl.shape[0], xm.shape[0], top.shape[0]
    loads = [
        pltpu.make_async_copy(src.at[0], dst, load_sems.at[i])
        for i, (src, dst) in enumerate((
            (inv_leaf, il), (rhs_leaf, rl), (off_leaf_mid, lm), (inv_mid, im), (rhs_mid, rm),
            (off_leaf_top, lt), (off_mid_top, mt),
        ))
    ]
    for load in loads:
        load.start()

    def clear(s, carry):
        top[s] = jnp.zeros(top.shape[1:], top.dtype)
        return carry

    lax.fori_loop(0, tops, clear, 0)

    parents = [lax.rem(parent_leaf[0, k], mids) for k in range(leaves)]
    first, last = [], []
    for j in range(mids):
        low = jnp.int32(0)
        high = jnp.int32(0)
        for k in range(leaves):
            high = jnp.where(parents[k] == j, k, high)
            back = leaves - 1 - k
            low = jnp.where(parents[back] == j, back, low)
        first.append(low)
        last.append(high)

    loads[0].wait()
    loads[1].wait()
    for k in range(leaves):
        xl[k] = live_rows(dot(il[k], rl[k]), 0, width_leaf[0, k]).astype(BF16)
    store_leaf = pltpu.make_async_copy(xl, leaf_out.at[0], store_sems.at[0])
    store_leaf.start()

    for load in loads[2:5]:
        load.wait()
    for j in range(mids):
        total = dot(lm[first[j]], xl[first[j]]) + dot(lm[last[j]], xl[last[j]])
        mid_input = (rm[j].astype(F32) - total).astype(BF16)
        xm[j] = live_rows(dot(im[j], mid_input), 0, width_mid[0, j]).astype(BF16)
    store_mid = pltpu.make_async_copy(xm, mid_out.at[0], store_sems.at[1])
    store_mid.start()

    for load in loads[5:]:
        load.wait()
    for j in range(mids):
        low, high = first[j], last[j]
        update = dot(mt[j], xm[j])
        update += dot(lt[low], flagged(xl[low], pattern_leaf[0, low]))
        update += dot(lt[high], flagged(xl[high], pattern_leaf[0, high]))
        s = lax.rem(parent_mid[0, j], tops)
        top[s] = (top[s].astype(F32) + update).astype(BF16)
    store_top = pltpu.make_async_copy(top, top_out, store_sems.at[2])
    store_top.start()
    store_leaf.wait()
    store_mid.wait()
    store_top.wait()


def upper_kernel(
    nz, nx, ny,
    width_top, pattern_leaf, pattern_mid,
    updates, leaf_x, mid_x, off_leaf_out, off_mid_out, rhs_top, inv_top, off_top_out,
    top_solution, outer_out,
    t_own, t_rx, t_sum, a_rx, b_rx, a_sum, b_sum, a_rx2, b_rx2, top_in, inv, rhs, solved, sol_v,
    xl, xm, ol, om, ot,
    o_t, o_rx, o_s, o_rz, o_z, o_rx2, o_x, o_ry, o_fin,
    q_t, q_ry, q_z, q_rz, out_v,
    load_sems, core_s, core_r, pre_s, pre_r, a_s, a_r, b_s, b_r, a2_s, a2_r, b2_s, b2_r,
    g_s, g_r, f_s, f_r, oz_s, oz_r, ox_s, ox_r, oy_s, oy_r, qy_s, qy_r, qz_s, qz_r,
):
    z = lax.axis_index("pr")
    pc = lax.axis_index("pc")
    y = lax.axis_index("gz")
    x = pc // 2
    c = pc % 2
    other = 1 - c
    sibling = 2 * x + other
    tops = rhs_top.shape[0]
    per_y = tops // ny
    half = t_own.shape[3] // LANES
    slab = rhs_top.shape[1]
    part = t_own.shape[2]
    half_rows = 2 * part
    chunk = q_z.shape[1]
    rows = outer_out.shape[1]
    wide = o_t.shape[3]

    def to(z_, pc_, y_):
        return (z_, pc_, y_)

    def remote(src, dst, send, recv, device):
        return pltpu.make_async_remote_copy(
            src_ref=src, dst_ref=dst, send_sem=send, recv_sem=recv,
            device_id=device, device_id_type=MESH_IDS,
        )

    barrier = pltpu.get_barrier_semaphore()
    partners = [to(z, lax.rem(pc + d, 2 * nx), y) for d in range(1, 2 * nx)]
    partners += [to(z, pc, lax.rem(y + d, ny)) for d in range(1, ny)]
    partners += [to(lax.rem(z + d, nz), pc, y) for d in range(1, nz)]
    for partner in partners:
        pl.semaphore_signal(barrier, inc=1, device_id=partner, device_id_type=MESH_IDS)

    own_first = pl.multiple_of(c * half_rows, half_rows)
    load_pairs = [
        (updates.at[:, pl.ds(pl.multiple_of(c * half_rows + p * part, part), part), :], t_own.at[p])
        for p in range(2)
    ] + [
        (leaf_x.at[0], xl), (mid_x.at[0], xm), (off_leaf_out.at[0], ol), (off_mid_out.at[0], om),
        (off_top_out.at[pl.ds(y * per_y, per_y)], ot),
    ]
    loads = [
        pltpu.make_async_copy(src, dst, load_sems.at[i]) for i, (src, dst) in enumerate(load_pairs)
    ]
    for i in (2, 3, 0, 4, 5, 1, 6):
        loads[i].start()
    pl.semaphore_wait(barrier, len(partners))

    core_copies = [
        remote(
            updates.at[:, pl.ds(pl.multiple_of(other * half_rows + p * part, part), part), :],
            t_rx.at[p], core_s.at[p], core_r.at[p], to(z, sibling, y),
        )
        for p in range(2)
    ]
    for copy in core_copies:
        copy.start()

    slot = lax.rem(pc, nx)
    target_core = pc // nx
    pre_copies = []
    for d in range(nx):
        tx = lax.rem(x + d, nx)
        s = y * per_y + tx // half
        column = pl.multiple_of(lax.rem(tx, half) * LANES, LANES)
        pairs = (
            (inv_top.at[s], inv.at[slot]),
            (rhs_top.at[s, :, pl.ds(column, LANES)], rhs.at[slot]),
        )
        for i, (src, dst) in enumerate(pairs):
            copy = remote(
                src, dst, pre_s.at[i, d], pre_r.at[i, slot], to(z, 2 * tx + target_core, y)
            )
            pre_copies.append((d, copy))
            if d == 0:
                @pl.when(target_core == c)
                def _():
                    pltpu.make_async_copy(src, dst, pre_r.at[i, slot]).start()

                @pl.when(target_core != c)
                def _():
                    copy.start()
            else:
                copy.start()

    loads[2].wait()
    loads[3].wait()
    for k in range(xl.shape[0]):
        xl[k] = flagged(xl[k], pattern_leaf[1, k])
    for j in range(xm.shape[0]):
        xm[j] = flagged(xm[j], pattern_mid[0, j])
    loads[4].wait()
    loads[5].wait()

    def outer_rows(i, carry):
        first = pl.multiple_of(i * 2 * rows, 2 * rows)
        block = pl.ds(first, 2 * rows)
        total = jnp.zeros((2 * rows, xl.shape[2]), F32)
        for k in range(xl.shape[0]):
            total += dot(ol[k, block, :], xl[k])
        for j in range(xm.shape[0]):
            total += dot(om[j, block, :], xm[j])
        for core in range(2):
            turned = total[core * rows:(core + 1) * rows].T
            o_t[core, i] = turned.reshape(nz, wide, rows).astype(BF16)
        return carry

    lax.fori_loop(0, nx // 2, outer_rows, 0)

    a_copies, b_copies = [], []
    for p in range(2):
        loads[p].wait()
        core_copies[p].wait_recv()

        def pair_sum(s, carry):
            total = (t_own[p, s].astype(F32) + t_rx[p, s].astype(F32)).astype(BF16)
            for h in range(half):
                t_sum[p, s // per_y, (s % per_y) * half + h] = total[:, h * LANES:(h + 1) * LANES]
            return carry

        lax.fori_loop(0, tops, pair_sum, 0)
        if p == 0:
            for d in range(1, nx):
                tx = lax.rem(x + d, nx)
                a_copies.append(remote(
                    t_sum.at[0, :, tx], a_rx.at[d - 1], a_s.at[d - 1], a_r.at[d - 1],
                    to(z, 2 * tx + c, y),
                ))
                a_copies[-1].start()
        else:
            for d in range(1, ny):
                ty = lax.rem(y + d, ny)
                b_copies.append(remote(
                    t_sum.at[1, ty], b_rx.at[d - 1], b_s.at[d - 1], b_r.at[d - 1], to(z, pc, ty),
                ))
                b_copies[-1].start()

    lax.fori_loop(nx // 2, nx, outer_rows, 0)
    o_core = remote(
        o_t.at[other], o_rx, core_s.at[2], core_r.at[2], to(z, sibling, y)
    )
    o_core.start()

    a2_copies, b2_copies = [], []
    for copy in a_copies:
        copy.wait_recv()
    for i in range(ny):
        total = t_sum[0, i, x].astype(F32)
        for d in range(nx - 1):
            total += a_rx[d, i].astype(F32)
        a_sum[i] = total.astype(BF16)
    for d in range(1, ny):
        ty = lax.rem(y + d, ny)
        a2_copies.append(remote(
            a_sum.at[ty], a_rx2.at[d - 1], a2_s.at[d - 1], a2_r.at[d - 1], to(z, pc, ty),
        ))
        a2_copies[-1].start()
    for copy in b_copies:
        copy.wait_recv()
    for i in range(nx):
        total = t_sum[1, y, i].astype(F32)
        for d in range(ny - 1):
            total += b_rx[d, i].astype(F32)
        b_sum[i] = total.astype(BF16)
    for d in range(1, nx):
        tx = lax.rem(x + d, nx)
        b2_copies.append(remote(
            b_sum.at[tx], b_rx2.at[d - 1], b2_s.at[d - 1], b2_r.at[d - 1], to(z, 2 * tx + c, y),
        ))
        b2_copies[-1].start()

    o_core.wait_recv()
    oz_copies = []

    def outer_pair(i, carry):
        o_s[i] = (o_t[c, i].astype(F32) + o_rx[i].astype(F32)).astype(BF16)
        return carry

    lax.fori_loop(0, nx, outer_pair, 0)
    for d in range(1, nz):
        tz = lax.rem(z + d, nz)
        oz_copies.append(remote(
            o_s.at[:, tz], o_rz.at[d - 1], oz_s.at[d - 1], oz_r.at[d - 1], to(tz, pc, y),
        ))
        oz_copies[-1].start()

    for i in range(nx):
        pre = [
            remote(inv_top.at[0], inv.at[i], pre_s.at[0, 0], pre_r.at[0, i], to(z, sibling, y)),
            remote(rhs_top.at[0, :, pl.ds(0, LANES)], rhs.at[i], pre_s.at[1, 0], pre_r.at[1, i],
                   to(z, sibling, y)),
        ]
        for copy in pre:
            copy.wait_recv()
    right = rhs[...].reshape(half_rows, LANES).astype(F32)
    for copy in a2_copies:
        copy.wait_recv()
    total = a_sum[y].astype(F32)
    for d in range(ny - 1):
        total += a_rx2[d].astype(F32)
    top_in[c, pl.ds(0, part), :] = (right[:part] - total).astype(BF16)
    for copy in b2_copies:
        copy.wait_recv()
    total = b_sum[x].astype(F32)
    for d in range(nx - 1):
        total += b_rx2[d].astype(F32)
    top_in[c, pl.ds(part, part), :] = (right[part:] - total).astype(BF16)
    in_copy = remote(top_in.at[c], top_in.at[c], core_s.at[3], core_r.at[3], to(z, sibling, y))
    in_copy.start()
    in_copy.wait_recv()

    block = dot(inv[...].reshape(half_rows, inv.shape[2]), top_in[...].reshape(2 * half_rows, LANES))
    width = width_top[y * per_y + x // half]
    solved[x, c] = live_rows(block, c * half_rows, width).astype(BF16)

    g_copies, f_copies = [], []
    for d in range(1, nx):
        tx = lax.rem(x + d, nx)
        g_copies.append(remote(
            solved.at[x, c], solved.at[x, c], g_s.at[d - 1], g_r.at[d - 1], to(z, 2 * tx + c, y),
        ))
        g_copies[-1].start()
    f_copies.append(remote(
        solved.at[x, c], solved.at[x, c], f_s.at[0], f_r.at[0], to(z, sibling, y)
    ))
    f_copies[-1].start()

    for copy in oz_copies:
        copy.wait_recv()
    ox_copies = []
    for i in range(nx):
        total = o_s[i, z].astype(F32)
        for d in range(nz - 1):
            total += o_rz[d, i].astype(F32)
        o_z[i] = total.astype(BF16)
    for d in range(1, nx):
        tx = lax.rem(x + d, nx)
        ox_copies.append(remote(
            o_z.at[tx], o_rx2.at[d - 1], ox_s.at[d - 1], ox_r.at[d - 1], to(z, 2 * tx + c, y),
        ))
        ox_copies[-1].start()

    for d in range(1, nx):
        sx = lax.rem(x + nx - d, nx)
        g_copies[d - 1].wait_recv()
        f_copies.append(remote(
            solved.at[sx, c], solved.at[sx, c], f_s.at[d], f_r.at[d], to(z, sibling, y)
        ))
        f_copies[-1].start()

    for copy in ox_copies:
        copy.wait_recv()
    total = o_z[x].astype(F32)
    for d in range(nx - 1):
        total += o_rx2[d].astype(F32)
    o_x[...] = total.reshape(ny, chunk, rows)
    oy_copies = []
    for d in range(1, ny):
        ty = lax.rem(y + d, ny)
        oy_copies.append(remote(
            o_x.at[ty], o_ry.at[d - 1], oy_s.at[d - 1], oy_r.at[d - 1], to(z, pc, ty),
        ))
        oy_copies[-1].start()

    loads[6].wait()
    for copy in f_copies:
        copy.wait_recv()

    total = jnp.zeros((rows, half * LANES), F32)
    for t in range(per_y):
        blocks = [
            solved[t * half + h].reshape(2 * half_rows, LANES) for h in range(half)
        ]
        total += dot(ot[t], jnp.concatenate(blocks, axis=1))
    turned = total.T.reshape(nz, ny, chunk, rows)
    for i in range(ny):
        q_t[i] = turned[:, i].reshape(nz * chunk, rows).astype(BF16)
    qy_copies = []
    for d in range(1, ny):
        ty = lax.rem(y + d, ny)
        qy_copies.append(remote(
            q_t.at[ty], q_ry.at[d - 1], qy_s.at[d - 1], qy_r.at[d - 1], to(z, pc, ty),
        ))
        qy_copies[-1].start()

    for t in range(per_y):
        for h in range(half):
            sol_v[t, :, h * LANES:(h + 1) * LANES] = solved[
                t * half + h, pc // nx, pl.ds(pl.multiple_of(slot * slab, slab), slab), :
            ]
    store = pltpu.make_async_copy(sol_v, top_solution, load_sems.at[7])
    store.start()
    for copy in oy_copies:
        copy.wait_recv()
    total = o_x[y]
    for d in range(ny - 1):
        total += o_ry[d]
    o_fin[...] = total

    for copy in qy_copies:
        copy.wait_recv()
    total = q_t[y].astype(F32)
    for d in range(ny - 1):
        total += q_ry[d].astype(F32)
    q_z[...] = total.reshape(nz, chunk, rows)
    qz_copies = []
    for d in range(1, nz):
        tz = lax.rem(z + d, nz)
        qz_copies.append(remote(
            q_z.at[tz], q_rz.at[d - 1], qz_s.at[d - 1], qz_r.at[d - 1], to(tz, pc, y),
        ))
        qz_copies[-1].start()
    for copy in (
        core_copies + [o_core, in_copy] + a_copies + b_copies + a2_copies + b2_copies
        + g_copies + f_copies + oz_copies + ox_copies + oy_copies + qy_copies
    ):
        copy.wait_send()
    for d, copy in pre_copies:
        if d == 0:
            @pl.when(target_core != c)
            def _():
                copy.wait_send()
        else:
            copy.wait_send()
    store.wait()
    for copy in qz_copies:
        copy.wait_recv()
    total = q_z[z] + o_fin[...]
    for d in range(nz - 1):
        total += q_rz[d]
    out_v[...] = total
    last = pltpu.make_async_copy(out_v, outer_out, load_sems.at[8])
    last.start()
    for copy in qz_copies:
        copy.wait_send()
    last.wait()


def on_device(
    nz, nx, ny,
    rhs_leaf, rhs_mid, rhs_top, inv_leaf, inv_mid, inv_top,
    off_leaf_mid, off_leaf_top, off_leaf_out, off_mid_top, off_mid_out, off_top_out,
    parent_leaf, parent_mid, width_leaf, width_mid, width_top, pattern_leaf, pattern_mid,
):
    smem = pl.BlockSpec(memory_space=pltpu.SMEM)
    hbm = pl.BlockSpec(memory_space=pl.ANY)
    leaves, leaf_w, num_rhs = rhs_leaf.shape[1:]
    mids, mid_w = rhs_mid.shape[1:3]
    tops, slab = rhs_top.shape[:2]
    top_w = inv_top.shape[2]
    outer = off_leaf_out.shape[2]
    rows = off_top_out.shape[1]
    half = num_rhs // LANES
    per_y = tops // ny
    assert per_y * half == nx and slab * 2 * nx == top_w and rows * 2 * nx == outer
    pattern = jnp.transpose(pattern_leaf[0], (1, 0))
    parents_l = parent_leaf.reshape(1, leaves)
    parents_m = parent_mid.reshape(1, mids)

    def vm(*shape, dtype=BF16):
        return pltpu.VMEM(shape, dtype)

    leaf_x, mid_x, updates = pl.pallas_call(
        subtree_kernel,
        out_shape=(
            jax.ShapeDtypeStruct(rhs_leaf.shape, BF16),
            jax.ShapeDtypeStruct(rhs_mid.shape, BF16),
            jax.ShapeDtypeStruct((tops, top_w, num_rhs), BF16),
        ),
        in_specs=[smem] * 5 + [hbm] * 7,
        out_specs=(hbm,) * 3,
        scratch_shapes=[
            vm(leaves, leaf_w, num_rhs), vm(leaves, leaf_w, leaf_w), vm(leaves, mid_w, leaf_w),
            vm(mids, mid_w, num_rhs), vm(mids, mid_w, mid_w),
            vm(leaves, top_w, leaf_w), vm(mids, top_w, mid_w),
            vm(leaves, leaf_w, num_rhs), vm(mids, mid_w, num_rhs), vm(tops, top_w, num_rhs),
            pltpu.SemaphoreType.DMA((7,)), pltpu.SemaphoreType.DMA((3,)),
        ],
        compiler_params=pltpu.CompilerParams(vmem_limit_bytes=60 << 20),
        name="subtrees",
    )(
        parents_l, parents_m, width_leaf, width_mid, pattern,
        rhs_leaf, inv_leaf, off_leaf_mid, rhs_mid, inv_mid, off_leaf_top, off_mid_top,
    )

    half_rows = top_w // 2
    part = half_rows // 2
    wide = num_rhs // nz
    chunk = wide // ny
    sems = pltpu.SemaphoreType.DMA
    top_solution, outer_part = pl.pallas_call(
        functools.partial(upper_kernel, nz, nx, ny),
        out_shape=(
            jax.ShapeDtypeStruct((per_y, slab, num_rhs), BF16),
            jax.ShapeDtypeStruct((chunk, rows), F32),
        ),
        in_specs=[smem] * 3 + [hbm] * 8,
        out_specs=(hbm, hbm),
        scratch_shapes=[
            vm(2, tops, part, num_rhs), vm(2, tops, part, num_rhs),
            vm(2, ny, nx, part, LANES),
            vm(nx - 1, ny, part, LANES), vm(ny - 1, nx, part, LANES),
            vm(ny, part, LANES), vm(nx, part, LANES),
            vm(ny - 1, part, LANES), vm(nx - 1, part, LANES),
            vm(2, half_rows, LANES), vm(nx, slab, top_w), vm(nx, slab, LANES),
            vm(nx, 2, half_rows, LANES), vm(per_y, slab, num_rhs),
            vm(leaves, leaf_w, num_rhs), vm(mids, mid_w, num_rhs),
            vm(leaves, outer, leaf_w), vm(mids, outer, mid_w), vm(per_y, rows, top_w),
            vm(2, nx, nz, wide, rows), vm(nx, nz, wide, rows), vm(nx, nz, wide, rows),
            vm(nz - 1, nx, wide, rows), vm(nx, wide, rows), vm(nx - 1, wide, rows),
            vm(ny, chunk, rows, dtype=F32), vm(ny - 1, chunk, rows, dtype=F32),
            vm(chunk, rows, dtype=F32),
            vm(ny, nz * chunk, rows), vm(ny - 1, nz * chunk, rows),
            vm(nz, chunk, rows, dtype=F32), vm(nz - 1, chunk, rows, dtype=F32),
            vm(chunk, rows, dtype=F32),
            sems((9,)), sems((4,)), sems((4,)), sems((2, nx)), sems((2, nx)),
            sems((nx - 1,)), sems((nx - 1,)), sems((ny - 1,)), sems((ny - 1,)),
            sems((ny - 1,)), sems((ny - 1,)), sems((nx - 1,)), sems((nx - 1,)),
            sems((nx - 1,)), sems((nx - 1,)), sems((nx,)), sems((nx,)),
            sems((nz - 1,)), sems((nz - 1,)), sems((nx - 1,)), sems((nx - 1,)),
            sems((ny - 1,)), sems((ny - 1,)), sems((ny - 1,)), sems((ny - 1,)),
            sems((nz - 1,)), sems((nz - 1,)),
        ],
        compiler_params=pltpu.CompilerParams(
            collective_id=0, has_side_effects=True, vmem_limit_bytes=60 << 20
        ),
        name="upper",
    )(
        width_top, pattern, pattern_mid,
        updates, leaf_x, mid_x, off_leaf_out, off_mid_out, rhs_top, inv_top, off_top_out,
    )
    return leaf_x, mid_x, top_solution, outer_part.T


def solution(mesh):
    sizes = dict(mesh.shape)
    deep = P("gz", ("pr", "pc"), None, None)
    flat = P("pr", "pc", None)
    return jax.shard_map(
        functools.partial(on_device, sizes["pr"], sizes["pc"] // 2, sizes["gz"]),
        mesh=mesh,
        in_specs=(
            deep, deep, flat, deep, deep, flat,
            deep, deep, deep, deep, deep, flat,
            P("gz", ("pr", "pc"), None),
            P("gz", ("pr", "pc"), None),
            P("gz", ("pr", "pc")),
            P("gz", ("pr", "pc")),
            P("pr"),
            P("gz", ("pr", "pc"), None),
            P("gz", ("pr", "pc")),
        ),
        out_specs=(deep, deep, P(("pr", "gz"), "pc", None), P("pc", ("pr", "gz"))),
        check_vma=False,
    )
```

time: 365 us -> 53.5 us (0.15)
  the two profiles are of different devices: /device:TPU:1 before, /device:TPU:32 now
where the time goes in v1:
time: 53.5 us; the launch traced here: 53.3 us
  Pallas kernels  49.9 us (93%)
  local copies, waits for them, and re-layouts  2.75 us (5%)
  between operations  0.65 us (1%)
    pallas_call x1, Pallas kernels, on_device(): pl.pallas_call(functools.partial(upper_kernel, nz, nx, ny), out_shape=(ja...  43.6 us
    pallas_call x1, Pallas kernels, on_device(): pl.pallas_call(subtree_kernel, out_shape=(jax.ShapeDtypeStruct(rhs_leaf.s...  6.27 us
    unnamed x2, local copies, waits for them, and re-layouts  2.75 us

profile of v1, /device:TPU:32, one launch (start us, length us, event | category | flops | bytes accessed | tf_op | source)
XLA Modules:
  0.0 53.3 jit_solution(16515789614724206606)
XLA Ops:
  0.6 6.3 %subtrees.1 = (bf16[1,8,128,256]{3,2,1,0:T(8,128)(2,1)}, bf16[1,4,256,256]{3,2,1,0:T(8,128)(2,1)}, bf16[8,512,256]{2,1,0:T(8,128)(2,1)}) custom-call(s32[1,8]{1,0:T(1,128)} %bitcast.9, s32[1,4]{1,0:T(1,128)} %bitcast.10, s32[1,8]{1,0:T(1,128)} %width_leaf.1, s32[1,4]{1,0:T(1,128)} %width_mid.1, s32[2,8]{1,0:T(2,128)} %bitcast.6, ...), custom_call_target="tpu_custom_call" | custom-call | tf_op jit(solution)/shard_map/subtrees/pallas_call | solution.py:470
  6.9 43.6 %upper.1 = (bf16[2,64,256]{2,1,0:T(8,128)(2,1)}, f32[8,128]{1,0:T(8,128)}) custom-call(s32[8]{0:T(128)} %width_top.1, s32[2,8]{1,0:T(2,128)} %bitcast.7, s32[1,4]{1,0:T(1,128)} %pattern_mid.1, bf16[8,512,256]{2,1,0:T(8,128)(2,1)} %get-tuple-element.11.updates, bf16[1,8,128,256]{3,2,1,0:T(8,128)(2,1)} %get-tuple-element.18.leaf_x, ...), custom_call_target="tpu_custom_call" | custom-call | tf_op jit(solution)/shard_map/upper/pallas_call | solution.py:498
  50.5 1.5 %copy.25 = bf16[2,64,256]{2,1,0:T(8,128)(2,1)} copy(bf16[2,64,256]{2,1,0:T(8,128)(2,1)} %get-tuple-element.20) | data formatting | bytes 131072
  52.0 1.3 %copy.26 = f32[128,8]{0,1:T(8,128)} copy(f32[128,8]{0,1:T(8,128)} %bitcast.8) | data formatting | bytes 8192

commit v2 on v1

v2 whole, which is shorter than its diff:
```python
import functools

import jax
import jax.numpy as jnp
from jax import lax
from jax.experimental import pallas as pl
from jax.experimental.pallas import tpu as pltpu
from jax.sharding import PartitionSpec as P

MESH_IDS = pl.DeviceIdType.MESH
F32 = jnp.float32
BF16 = jnp.bfloat16
LANES = 128


def dot(a, b):
    return jnp.dot(a, b, preferred_element_type=F32)


def live_rows(values, first_row, width):
    row_ids = first_row + lax.broadcasted_iota(jnp.int32, values.shape, 0)
    return jnp.where(row_ids < width, values, 0.0)


def flagged(values, flag):
    return jnp.where(flag != 0, values, jnp.zeros_like(values))


def dot_nt(a, b):
    return lax.dot_general(a, b, (((1,), (1,)), ((), ())), preferred_element_type=F32)


def window_kernel(
    nz, nx, ny,
    parent_leaf, parent_mid, width_leaf, width_mid, width_top, pattern_leaf, pattern_mid,
    rhs_leaf, rhs_mid, rhs_top, inv_leaf, inv_mid, inv_top,
    off_leaf_mid, off_leaf_top, off_leaf_out, off_mid_top, off_mid_out, off_top_out,
    leaf_out, mid_out, top_solution, outer_out,
    rl, il, lm, rm, im, lt, mt, xl, xm, ol, om, xo, up_own, up_rx, mask, mask_rx,
    t_sum, a_rx, b_rx, a_sum, b_sum, a_rx2, b_rx2, top_in, inv, rhs,
    unit, sol_rx, sol_v, turned, gathered, wt,
    o_t, o_rx, o_s, o_rz, o_z, o_rx2, o_x, o_ry, o_fin, q, q_rx, out_v,
    load_sems, store_sems, core_s, core_r, pre_s, pre_r, a_s, a_r, b_s, b_r, a2_s, a2_r, b2_s, b2_r,
    sol_s, sol_r, g_s, g_r, oz_s, oz_r, ox_s, ox_r, oy_s, oy_r, q_s, q_r,
):
    z = lax.axis_index("pr")
    pc = lax.axis_index("pc")
    y = lax.axis_index("gz")
    x = pc // 2
    c = pc % 2
    other = 1 - c
    sibling = 2 * x + other
    leaves, mids = xl.shape[0], xm.shape[0]
    tops = rhs_top.shape[0]
    per_y = tops // ny
    half = xl.shape[2] // LANES
    slab = rhs_top.shape[1]
    part = t_sum.shape[3]
    half_rows = 2 * part
    chunk = q.shape[2]
    rows = outer_out.shape[1]
    wide = o_t.shape[3]
    group = gathered.shape[2]
    num_rhs = xl.shape[2]

    def remote(src, dst, send, recv, device):
        return pltpu.make_async_remote_copy(
            src_ref=src, dst_ref=dst, send_sem=send, recv_sem=recv,
            device_id=device, device_id_type=MESH_IDS,
        )

    barrier = pltpu.get_barrier_semaphore()
    partners = [(z, lax.rem(pc + d, 2 * nx), y) for d in range(1, 2 * nx)]
    for dy in range(1, ny):
        for dx in range(nx):
            partners.append((z, lax.rem(pc + 2 * dx, 2 * nx), lax.rem(y + dy, ny)))
    for dz in range(1, nz):
        for core in range(2):
            partners.append((lax.rem(z + dz, nz), 2 * x + core, y))
    for partner in partners:
        pl.semaphore_signal(barrier, inc=1, device_id=partner, device_id_type=MESH_IDS)

    load_pairs = [
        (inv_leaf.at[0], il), (rhs_leaf.at[0], rl), (off_leaf_mid.at[0], lm),
        (inv_mid.at[0], im), (rhs_mid.at[0], rm), (off_mid_top.at[0], mt), (off_leaf_top.at[0], lt),
        (off_leaf_out.at[0], ol), (off_mid_out.at[0], om),
        (off_top_out.at[:, :, pl.ds(pl.multiple_of(c * half_rows, half_rows), half_rows)], wt.at[:, c]),
    ]
    loads = [
        pltpu.make_async_copy(src, dst, load_sems.at[i]) for i, (src, dst) in enumerate(load_pairs)
    ]
    for load in loads[:7]:
        load.start()

    parents = [lax.rem(parent_leaf[0, k], mids) for k in range(leaves)]
    first, last = [], []
    for j in range(mids):
        low = jnp.int32(0)
        high = jnp.int32(0)
        for k in range(leaves):
            high = jnp.where(parents[k] == j, k, high)
            back = leaves - 1 - k
            low = jnp.where(parents[back] == j, back, low)
        first.append(low)
        last.append(high)
    for j in range(mids):
        ids = lax.broadcasted_iota(jnp.int32, mask.shape[1:], 0)
        mask[j] = jnp.where(ids == lax.rem(parent_mid[0, j], tops), 1.0, 0.0)

    loads[0].wait()
    loads[1].wait()
    for k in range(leaves):
        xl[k] = live_rows(dot(il[k], rl[k]), 0, width_leaf[0, k]).astype(BF16)
    store_leaf = pltpu.make_async_copy(xl, leaf_out.at[0], store_sems.at[0])
    store_leaf.start()

    for load in loads[2:5]:
        load.wait()
    for j in range(mids):
        total = dot(
            jnp.concatenate([lm[first[j]], lm[last[j]]], axis=1),
            jnp.concatenate([xl[first[j]], xl[last[j]]], axis=0),
        )
        mid_input = (rm[j].astype(F32) - total).astype(BF16)
        xm[j] = live_rows(dot(im[j], mid_input), 0, width_mid[0, j]).astype(BF16)
    store_mid = pltpu.make_async_copy(xm, mid_out.at[0], store_sems.at[1])
    store_mid.start()

    pl.semaphore_wait(barrier, len(partners))
    mask_copy = remote(mask, mask_rx, core_s.at[0], core_r.at[0], (z, sibling, y))
    mask_copy.start()

    slot = lax.rem(pc, nx)
    target_core = pc // nx
    pre_copies = []
    for d in range(nx):
        tx = lax.rem(x + d, nx)
        s = y * per_y + tx // half
        column = pl.multiple_of(lax.rem(tx, half) * LANES, LANES)
        pairs = (
            (inv_top.at[s], inv.at[slot]),
            (rhs_top.at[s, :, pl.ds(column, LANES)], rhs.at[slot]),
        )
        for i, (src, dst) in enumerate(pairs):
            copy = remote(
                src, dst, pre_s.at[i, d], pre_r.at[i, slot], (z, 2 * tx + target_core, y)
            )
            pre_copies.append((d, copy))
            if d == 0:
                @pl.when(target_core == c)
                def _():
                    pltpu.make_async_copy(src, dst, pre_r.at[i, slot]).start()

                @pl.when(target_core != c)
                def _():
                    copy.start()
            else:
                copy.start()

    loads[5].wait()
    loads[6].wait()
    up_copies = []
    for j in range(mids):
        low, high = first[j], last[j]
        update = dot(
            jnp.concatenate([mt[j], lt[low], lt[high]], axis=1),
            jnp.concatenate([
                xm[j], flagged(xl[low], pattern_leaf[0, low]), flagged(xl[high], pattern_leaf[0, high])
            ], axis=0),
        )
        up_own[j] = update.astype(BF16)
        up_copies.append(remote(
            up_own.at[j, pl.ds(pl.multiple_of(other * half_rows, half_rows), half_rows), :],
            up_rx.at[j], core_s.at[1 + j], core_r.at[1 + j], (z, sibling, y),
        ))
        up_copies[-1].start()
    for load in loads[7:]:
        load.start()
    w_copy = remote(
        off_top_out.at[:, :, pl.ds(pl.multiple_of(other * half_rows, half_rows), half_rows)],
        wt.at[:, c], core_s.at[1 + mids], core_r.at[1 + mids], (z, sibling, y),
    )

    mask_copy.wait_recv()
    for copy in up_copies:
        copy.wait_recv()
    step = 16
    a_copies, b_copies = [], []
    for p in range(2):
        def pair_sum(i, carry):
            at = pl.multiple_of(i * step, step)
            mine = pl.ds(pl.multiple_of(c * half_rows + p * part + at, step), step)
            theirs = pl.ds(pl.multiple_of(p * part + at, step), step)
            blocks = [up_own[j, mine, :].astype(F32) for j in range(mids)]
            blocks += [up_rx[j, theirs, :].astype(F32) for j in range(mids)]
            for s in range(tops):
                for h in range(half):
                    total = jnp.zeros((step, LANES), F32)
                    for j in range(2 * mids):
                        table = mask if j < mids else mask_rx
                        weight = table[j % mids, s:s + 1, :]
                        total += weight * blocks[j][:, h * LANES:(h + 1) * LANES]
                    t_sum[p, s // per_y, (s % per_y) * half + h, pl.ds(at, step), :] = total.astype(BF16)
            return carry

        lax.fori_loop(0, part // step, pair_sum, 0)
        if p == 0:
            for d in range(1, nx):
                tx = lax.rem(x + d, nx)
                a_copies.append(remote(
                    t_sum.at[0, :, tx], a_rx.at[d - 1], a_s.at[d - 1], a_r.at[d - 1],
                    (z, 2 * tx + c, y),
                ))
                a_copies[-1].start()
        else:
            for d in range(1, ny):
                ty = lax.rem(y + d, ny)
                b_copies.append(remote(
                    t_sum.at[1, ty], b_rx.at[d - 1], b_s.at[d - 1], b_r.at[d - 1], (z, pc, ty),
                ))
                b_copies[-1].start()
    w_copy.start()

    leaf_w, mid_w = xl.shape[1], xm.shape[1]
    for k in range(leaves):
        xo[k * leaf_w:(k + 1) * leaf_w] = flagged(xl[k], pattern_leaf[1, k])
    base = leaves * leaf_w
    for j in range(mids):
        xo[base + j * mid_w:base + (j + 1) * mid_w] = flagged(xm[j], pattern_mid[0, j])
    loads[7].wait()
    loads[8].wait()

    def outer_rows(i, carry):
        block = pl.ds(pl.multiple_of(i * 2 * rows, 2 * rows), 2 * rows)
        total = dot(
            jnp.concatenate(
                [ol[k, block, :] for k in range(leaves)] + [om[j, block, :] for j in range(mids)],
                axis=1,
            ),
            xo[...],
        )
        for core in range(2):
            across = total[core * rows:(core + 1) * rows].T
            o_t[core, i] = across.reshape(nz, wide, rows).astype(BF16)
        return carry

    lax.fori_loop(0, nx, outer_rows, 0)
    o_core = remote(
        o_t.at[other], o_rx, core_s.at[2 + mids], core_r.at[2 + mids], (z, sibling, y)
    )
    o_core.start()

    a2_copies, b2_copies = [], []
    for copy in a_copies:
        copy.wait_recv()
    for i in range(ny):
        total = t_sum[0, i, x].astype(F32)
        for d in range(nx - 1):
            total += a_rx[d, i].astype(F32)
        a_sum[i] = total.astype(BF16)
    for d in range(1, ny):
        ty = lax.rem(y + d, ny)
        a2_copies.append(remote(
            a_sum.at[ty], a_rx2.at[d - 1], a2_s.at[d - 1], a2_r.at[d - 1], (z, pc, ty),
        ))
        a2_copies[-1].start()
    for copy in b_copies:
        copy.wait_recv()
    for i in range(nx):
        total = t_sum[1, y, i].astype(F32)
        for d in range(ny - 1):
            total += b_rx[d, i].astype(F32)
        b_sum[i] = total.astype(BF16)
    for d in range(1, nx):
        tx = lax.rem(x + d, nx)
        b2_copies.append(remote(
            b_sum.at[tx], b_rx2.at[d - 1], b2_s.at[d - 1], b2_r.at[d - 1], (z, 2 * tx + c, y),
        ))
        b2_copies[-1].start()

    o_core.wait_recv()
    oz_copies = []

    def outer_pair(i, carry):
        o_s[i] = (o_t[c, i].astype(F32) + o_rx[i].astype(F32)).astype(BF16)
        return carry

    lax.fori_loop(0, nx, outer_pair, 0)
    for d in range(1, nz):
        tz = lax.rem(z + d, nz)
        oz_copies.append(remote(
            o_s.at[:, tz], o_rz.at[d - 1], oz_s.at[d - 1], oz_r.at[d - 1], (tz, pc, y),
        ))
        oz_copies[-1].start()

    for i in range(nx):
        pre = [
            remote(inv_top.at[0], inv.at[i], pre_s.at[0, 0], pre_r.at[0, i], (z, sibling, y)),
            remote(rhs_top.at[0, :, pl.ds(0, LANES)], rhs.at[i], pre_s.at[1, 0], pre_r.at[1, i],
                   (z, sibling, y)),
        ]
        for copy in pre:
            copy.wait_recv()
    right = rhs[...].reshape(half_rows, LANES).astype(F32)
    for copy in a2_copies:
        copy.wait_recv()
    total = a_sum[y].astype(F32)
    for d in range(ny - 1):
        total += a_rx2[d].astype(F32)
    top_in[c, pl.ds(0, part), :] = (right[:part] - total).astype(BF16)
    for copy in b2_copies:
        copy.wait_recv()
    total = b_sum[x].astype(F32)
    for d in range(nx - 1):
        total += b_rx2[d].astype(F32)
    top_in[c, pl.ds(part, part), :] = (right[part:] - total).astype(BF16)
    in_copy = remote(
        top_in.at[c], top_in.at[c], core_s.at[3 + mids], core_r.at[3 + mids], (z, sibling, y)
    )
    in_copy.start()
    in_copy.wait_recv()

    block = dot(inv[...].reshape(half_rows, inv.shape[2]), top_in[...].reshape(2 * half_rows, LANES))
    block = live_rows(block, c * half_rows, width_top[y * per_y + x // half])
    across = block.T.reshape(nz // half, ny, chunk, half_rows)
    for i in range(ny):
        turned[i] = across[:, i].reshape(group, half_rows).astype(BF16)
    unit[...] = block.reshape(nx, slab, LANES).astype(BF16)

    g_copies = []
    for dy in range(ny):
        for dx in range(nx):
            if dx or dy:
                tx = lax.rem(x + dx, nx)
                ty = lax.rem(y + dy, ny)
                i = dy * nx + dx - 1
                g_copies.append(remote(
                    turned.at[ty], gathered.at[y, x], g_s.at[i], g_r.at[i], (z, 2 * tx + c, ty),
                ))
                g_copies[-1].start()
    gathered[y, x] = turned[y]

    sol_copies = []
    for d in range(nx):
        i = lax.rem(slot + d, nx)
        copy = remote(
            unit.at[i], sol_rx.at[x], sol_s.at[d], sol_r.at[x], (z, nx * c + i, y)
        )
        sol_copies.append((d, copy))
        if d == 0:
            @pl.when(target_core == c)
            def _():
                pltpu.make_async_copy(unit.at[i], sol_rx.at[x], sol_r.at[x]).start()

            @pl.when(target_core != c)
            def _():
                copy.start()
        else:
            copy.start()

    for copy in oz_copies:
        copy.wait_recv()
    ox_copies = []
    for i in range(nx):
        total = o_s[i, z].astype(F32)
        for d in range(nz - 1):
            total += o_rz[d, i].astype(F32)
        o_z[i] = total.astype(BF16)
    for d in range(1, nx):
        tx = lax.rem(x + d, nx)
        ox_copies.append(remote(
            o_z.at[tx], o_rx2.at[d - 1], ox_s.at[d - 1], ox_r.at[d - 1], (z, 2 * tx + c, y),
        ))
        ox_copies[-1].start()

    loads[9].wait()
    w_copy.wait_recv()
    for copy in g_copies:
        copy.wait_recv()

    total = jnp.zeros((half * group, 2 * rows), F32)
    for i in range(ny):
        for t in range(per_y):
            left = gathered[i, t * half:(t + 1) * half].reshape(half * group, half_rows)
            total += dot_nt(left, wt[i * per_y + t].reshape(2 * rows, half_rows))
    for core in range(2):
        q[core] = total[:, core * rows:(core + 1) * rows].reshape(nz, chunk, rows)
    q_copies = []
    for dz in range(nz):
        for dc in range(2):
            if dz or dc:
                tz = lax.rem(z + dz, nz)
                tc = lax.rem(c + dc, 2)
                i = 2 * dz + dc - 1
                q_copies.append(remote(
                    q.at[tc, tz], q_rx.at[i], q_s.at[i], q_r.at[i], (tz, 2 * x + tc, y),
                ))
                q_copies[-1].start()

    for copy in ox_copies:
        copy.wait_recv()
    total = o_z[x].astype(F32)
    for d in range(nx - 1):
        total += o_rx2[d].astype(F32)
    o_x[...] = total.reshape(ny, chunk, rows)
    oy_copies = []
    for d in range(1, ny):
        ty = lax.rem(y + d, ny)
        oy_copies.append(remote(
            o_x.at[ty], o_ry.at[d - 1], oy_s.at[d - 1], oy_r.at[d - 1], (z, pc, ty),
        ))
        oy_copies[-1].start()
    for i in range(nx):
        remote(unit.at[0], sol_rx.at[i], sol_s.at[0], sol_r.at[i], (z, sibling, y)).wait_recv()
    for t in range(per_y):
        for h in range(half):
            sol_v[t, :, h * LANES:(h + 1) * LANES] = sol_rx[t * half + h]
    store_sol = pltpu.make_async_copy(sol_v, top_solution, store_sems.at[2])
    store_sol.start()
    for copy in oy_copies:
        copy.wait_recv()
    total = o_x[y]
    for d in range(ny - 1):
        total += o_ry[d]
    o_fin[...] = total

    for copy in (
        [mask_copy, w_copy, o_core, in_copy] + up_copies + a_copies + b_copies + a2_copies
        + b2_copies + g_copies + oz_copies + ox_copies + oy_copies
    ):
        copy.wait_send()
    for d, copy in pre_copies + sol_copies:
        if d == 0:
            @pl.when(target_core != c)
            def _():
                copy.wait_send()
        else:
            copy.wait_send()
    store_leaf.wait()
    store_mid.wait()
    store_sol.wait()
    for copy in q_copies:
        copy.wait_recv()
    total = q[c, z] + o_fin[...]
    for d in range(2 * nz - 1):
        total += q_rx[d]
    out_v[...] = total
    last_store = pltpu.make_async_copy(out_v, outer_out, store_sems.at[3])
    last_store.start()
    for copy in q_copies:
        copy.wait_send()
    last_store.wait()


def finish_kernel(*refs):
    count = (len(refs) - 2) // 3
    ins, outs, held = refs[:count], refs[count:2 * count], refs[2 * count:3 * count]
    in_sems, out_sems = refs[-2:]
    loads = [
        pltpu.make_async_copy(ins[i], held[i], in_sems.at[i]) for i in range(count)
    ]
    stores = [
        pltpu.make_async_copy(held[i], outs[i], out_sems.at[i]) for i in range(count)
    ]
    for load in loads:
        load.start()
    for load, store in zip(loads, stores):
        load.wait()
        store.start()
    for store in stores:
        store.wait()


def on_device(
    nz, nx, ny,
    rhs_leaf, rhs_mid, rhs_top, inv_leaf, inv_mid, inv_top,
    off_leaf_mid, off_leaf_top, off_leaf_out, off_mid_top, off_mid_out, off_top_out,
    parent_leaf, parent_mid, width_leaf, width_mid, width_top, pattern_leaf, pattern_mid,
):
    smem = pl.BlockSpec(memory_space=pltpu.SMEM)
    hbm = pl.BlockSpec(memory_space=pl.ANY)
    leaves, leaf_w, num_rhs = rhs_leaf.shape[1:]
    mids, mid_w = rhs_mid.shape[1:3]
    tops, slab = rhs_top.shape[:2]
    top_w = inv_top.shape[2]
    outer = off_leaf_out.shape[2]
    rows = off_top_out.shape[1]
    half = num_rhs // LANES
    per_y = tops // ny
    assert per_y * half == nx and slab * 2 * nx == top_w and rows * 2 * nx == outer
    half_rows = top_w // 2
    part = half_rows // 2
    wide = num_rhs // nz
    chunk = wide // ny
    group = nz // half * chunk

    def vm(*shape, dtype=BF16):
        return pltpu.VMEM(shape, dtype)

    sems = pltpu.SemaphoreType.DMA
    results = pl.pallas_call(
        functools.partial(window_kernel, nz, nx, ny),
        out_shape=(
            jax.ShapeDtypeStruct(rhs_leaf.shape, BF16),
            jax.ShapeDtypeStruct(rhs_mid.shape, BF16),
            jax.ShapeDtypeStruct((per_y, slab, num_rhs), BF16),
            jax.ShapeDtypeStruct((chunk, rows), F32),
        ),
        in_specs=[smem] * 7 + [hbm] * 12,
        out_specs=(hbm,) * 4,
        scratch_shapes=[
            vm(leaves, leaf_w, num_rhs), vm(leaves, leaf_w, leaf_w), vm(leaves, mid_w, leaf_w),
            vm(mids, mid_w, num_rhs), vm(mids, mid_w, mid_w),
            vm(leaves, top_w, leaf_w), vm(mids, top_w, mid_w),
            vm(leaves, leaf_w, num_rhs), vm(mids, mid_w, num_rhs),
            vm(leaves, outer, leaf_w), vm(mids, outer, mid_w),
            vm(leaves * leaf_w + mids * mid_w, num_rhs),
            vm(mids, top_w, num_rhs), vm(mids, half_rows, num_rhs),
            vm(mids, max(tops, 8), LANES, dtype=F32), vm(mids, max(tops, 8), LANES, dtype=F32),
            vm(2, ny, nx, part, LANES),
            vm(nx - 1, ny, part, LANES), vm(ny - 1, nx, part, LANES),
            vm(ny, part, LANES), vm(nx, part, LANES),
            vm(ny - 1, part, LANES), vm(nx - 1, part, LANES),
            vm(2, half_rows, LANES), vm(nx, slab, top_w), vm(nx, slab, LANES),
            vm(nx, slab, LANES), vm(nx, slab, LANES), vm(per_y, slab, num_rhs),
            vm(ny, group, half_rows), vm(ny, nx, group, half_rows),
            vm(tops, 2, rows, half_rows),
            vm(2, nx, nz, wide, rows), vm(nx, nz, wide, rows), vm(nx, nz, wide, rows),
            vm(nz - 1, nx, wide, rows), vm(nx, wide, rows), vm(nx - 1, wide, rows),
            vm(ny, chunk, rows, dtype=F32), vm(ny - 1, chunk, rows, dtype=F32),
            vm(chunk, rows, dtype=F32),
            vm(2, nz, chunk, rows, dtype=F32), vm(2 * nz - 1, chunk, rows, dtype=F32),
            vm(chunk, rows, dtype=F32),
            sems((10,)), sems((4,)), sems((4 + mids,)), sems((4 + mids,)),
            sems((2, nx)), sems((2, nx)),
            sems((nx - 1,)), sems((nx - 1,)), sems((ny - 1,)), sems((ny - 1,)),
            sems((ny - 1,)), sems((ny - 1,)), sems((nx - 1,)), sems((nx - 1,)),
            sems((nx,)), sems((nx,)), sems((nx * ny - 1,)), sems((nx * ny - 1,)),
            sems((nz - 1,)), sems((nz - 1,)), sems((nx - 1,)), sems((nx - 1,)),
            sems((ny - 1,)), sems((ny - 1,)), sems((2 * nz - 1,)), sems((2 * nz - 1,)),
        ],
        compiler_params=pltpu.CompilerParams(
            collective_id=0, has_side_effects=True, vmem_limit_bytes=60 << 20
        ),
        name="window",
    )(
        parent_leaf.reshape(1, leaves), parent_mid.reshape(1, mids), width_leaf, width_mid,
        width_top, jnp.transpose(pattern_leaf[0], (1, 0)), pattern_mid,
        rhs_leaf, rhs_mid, rhs_top, inv_leaf, inv_mid, inv_top,
        off_leaf_mid, off_leaf_top, off_leaf_out, off_mid_top, off_mid_out, off_top_out,
    )
    leaf_x, mid_x, top_solution, outer_part = pl.pallas_call(
        finish_kernel,
        out_shape=tuple(jax.ShapeDtypeStruct(a.shape, a.dtype) for a in results),
        in_specs=[hbm] * 4,
        out_specs=(hbm,) * 4,
        scratch_shapes=[vm(*a.shape, dtype=a.dtype) for a in results] + [sems((4,)), sems((4,))],
        compiler_params=pltpu.CompilerParams(vmem_limit_bytes=60 << 20),
        name="finish",
    )(*results)
    return leaf_x, mid_x, top_solution, outer_part.T


def solution(mesh):
    sizes = dict(mesh.shape)
    deep = P("gz", ("pr", "pc"), None, None)
    flat = P("pr", "pc", None)
    return jax.shard_map(
        functools.partial(on_device, sizes["pr"], sizes["pc"] // 2, sizes["gz"]),
        mesh=mesh,
        in_specs=(
            deep, deep, flat, deep, deep, flat,
            deep, deep, deep, deep, deep, flat,
            P("gz", ("pr", "pc"), None),
            P("gz", ("pr", "pc"), None),
            P("gz", ("pr", "pc")),
            P("gz", ("pr", "pc")),
            P("pr"),
            P("gz", ("pr", "pc"), None),
            P("gz", ("pr", "pc")),
        ),
        out_specs=(deep, deep, P(("pr", "gz"), "pc", None), P("pc", ("pr", "gz"))),
        check_vma=False,
    )
```

time: 53.5 us -> 45.5 us (0.85)
  the two profiles are of different devices: /device:TPU:32 before, /device:TPU:1 now
where the time goes in v2:
time: 45.5 us; the launch traced here: 45.4 us
  Pallas kernels  44.7 us (98%)
  between operations  0.65 us (1%)
    pallas_call x1, Pallas kernels, on_device(): pl.pallas_call(functools.partial(window_kernel, nz, nx, ny), out_shape=(j...  42.7 us
    pallas_call x1, Pallas kernels, on_device(): pl.pallas_call(finish_kernel, out_shape=tuple((jax.ShapeDtypeStruct(a.sha...  2.09 us

profile of v2, /device:TPU:1, one launch (start us, length us, event | category | flops | bytes accessed | tf_op | source)
XLA Modules:
  0.0 45.4 jit_solution(7733826578363998455)
XLA Ops:
  0.6 42.7 %window.1 = (bf16[1,8,128,256]{3,2,1,0:T(8,128)(2,1)}, bf16[1,4,256,256]{3,2,1,0:T(8,128)(2,1)}, bf16[2,64,256]{2,1,0:T(8,128)(2,1)}, f32[8,128]{1,0:T(8,128)}) custom-call(s32[1,8]{1,0:T(1,128)} %bitcast.7, s32[1,4]{1,0:T(1,128)} %bitcast.8, s32[1,8]{1,0:T(1,128)} %width_leaf.1, s32[1,4]{1,0:T(1,128)} %width_mid.1, s32[8]{0:T(128)} %width_top.1, ...), custom_call_target="tpu_custom_call" | custom-call | tf_op jit(solution)/shard_map/window/pallas_call | solution.py:501
  43.3 2.1 %finish.1 = (bf16[1,8,128,256]{3,2,1,0:T(8,128)(2,1)}, bf16[1,4,256,256]{3,2,1,0:T(8,128)(2,1)}, bf16[2,64,256]{2,1,0:T(8,128)(2,1)}, f32[8,128]{1,0:T(8,128)}) custom-call(bf16[1,8,128,256]{3,2,1,0:T(8,128)(2,1)} %get-tuple-element.12.refs_0_, bf16[1,4,256,256]{3,2,1,0:T(8,128)(2,1)} %get-tuple-element.13.refs_1_, ...), custom_call_target="tpu_custom_call" | custom-call | tf_op jit(solution)/shard_map/finish/pallas_call | solution.py:552

commit v3 on v2

v3 whole, which is shorter than its diff:
```python
import functools

import jax
import jax.numpy as jnp
from jax import lax
from jax.experimental import pallas as pl
from jax.experimental.pallas import tpu as pltpu
from jax.sharding import PartitionSpec as P

MESH_IDS = pl.DeviceIdType.MESH
F32 = jnp.float32
BF16 = jnp.bfloat16
LANES = 128
CHUNKS = 2


def dot(a, b):
    return jnp.dot(a, b, preferred_element_type=F32)


def live_rows(values, first_row, width):
    row_ids = first_row + lax.broadcasted_iota(jnp.int32, values.shape, 0)
    return jnp.where(row_ids < width, values, 0.0)


def flagged(values, flag):
    return jnp.where(flag != 0, values, jnp.zeros_like(values))


def dot_nt(a, b):
    return lax.dot_general(a, b, (((1,), (1,)), ((), ())), preferred_element_type=F32)


def window_kernel(
    nz, nx, ny,
    parent_leaf_in, parent_mid_in, width_leaf_in, width_mid_in, width_top_in,
    pattern_leaf_in, pattern_mid_in,
    rhs_leaf, rhs_mid, rhs_top, inv_leaf, inv_mid, inv_top,
    off_leaf_mid, off_leaf_top, off_leaf_out, off_mid_top, off_mid_out, off_top_out,
    leaf_out, mid_out, top_solution, terms_out,
    parent_leaf, parent_mid, width_leaf, width_mid, width_top, pattern_leaf, pattern_mid,
    rl, il, lm, rm, im, lt, mt, xl, xm, ol, om, xo, xu, up_own, up_rx, mask, mask_rx,
    t_sum, a_rx, b_rx, a_sum, b_sum, a_rx2, b_rx2, top_in, inv, rhs,
    unit, sol_rx, sol_v, turned, gathered, wt,
    o_t, o_rx, o_s, o_rz, o_z, o_rx2, o_x, o_ry, q, own_v,
    vector_sems, load_sems, store_sems, core_s, core_r, pre_s, pre_r, a_s, a_r, b_s, b_r, a2_s, a2_r, b2_s, b2_r,
    sol_s, sol_r, g_s, g_r, oz_s, oz_r, ox_s, ox_r, oy_s, oy_r, q_s, q_r,
):
    z = lax.axis_index("pr")
    pc = lax.axis_index("pc")
    y = lax.axis_index("gz")
    x = pc // 2
    c = pc % 2
    other = 1 - c
    sibling = 2 * x + other
    leaves, mids = xl.shape[0], xm.shape[0]
    tops = rhs_top.shape[0]
    per_y = tops // ny
    half = xl.shape[2] // LANES
    slab = rhs_top.shape[1]
    chunks = t_sum.shape[0]
    part = t_sum.shape[4]
    block_rows = 2 * part
    half_rows = chunks * block_rows
    chunk = q.shape[2]
    rows = terms_out.shape[2]
    wide = o_t.shape[3]
    group = gathered.shape[2]
    num_rhs = xl.shape[2]

    def remote(src, dst, send, recv, device):
        return pltpu.make_async_remote_copy(
            src_ref=src, dst_ref=dst, send_sem=send, recv_sem=recv,
            device_id=device, device_id_type=MESH_IDS,
        )

    vectors = [
        pltpu.make_async_copy(src, dst, vector_sems.at[i]) for i, (src, dst) in enumerate((
            (width_leaf_in, width_leaf), (parent_leaf_in, parent_leaf), (parent_mid_in, parent_mid),
            (width_mid_in, width_mid), (pattern_leaf_in, pattern_leaf),
            (pattern_mid_in, pattern_mid), (width_top_in, width_top),
        ))
    ]
    load_pairs = [
        (inv_leaf.at[0], il), (rhs_leaf.at[0], rl), (off_leaf_mid.at[0], lm),
        (inv_mid.at[0], im), (rhs_mid.at[0], rm), (off_mid_top.at[0], mt), (off_leaf_top.at[0], lt),
        (off_leaf_out.at[0], ol), (off_mid_out.at[0], om),
        (off_top_out.at[:, :, pl.ds(pl.multiple_of(c * half_rows, half_rows), half_rows)], wt.at[:, c]),
    ]
    loads = [
        pltpu.make_async_copy(src, dst, load_sems.at[i]) for i, (src, dst) in enumerate(load_pairs)
    ]
    for load in loads[:2] + vectors + loads[2:7]:
        load.start()

    barrier = pltpu.get_barrier_semaphore()
    partners = [(z, lax.rem(pc + d, 2 * nx), y) for d in range(1, 2 * nx)]
    for dy in range(1, ny):
        for dx in range(nx):
            partners.append((z, lax.rem(pc + 2 * dx, 2 * nx), lax.rem(y + dy, ny)))
    for dz in range(1, nz):
        for core in range(2):
            partners.append((lax.rem(z + dz, nz), 2 * x + core, y))
    for partner in partners:
        pl.semaphore_signal(barrier, inc=1, device_id=partner, device_id_type=MESH_IDS)
    for vector in vectors:
        vector.wait()

    parents = [lax.rem(parent_leaf[0, k], mids) for k in range(leaves)]
    first, last = [], []
    for j in range(mids):
        low = jnp.int32(0)
        high = jnp.int32(0)
        for k in range(leaves):
            high = jnp.where(parents[k] == j, k, high)
            back = leaves - 1 - k
            low = jnp.where(parents[back] == j, back, low)
        first.append(low)
        last.append(high)
    for j in range(mids):
        ids = lax.broadcasted_iota(jnp.int32, mask.shape[1:], 0)
        mask[j] = jnp.where(ids == lax.rem(parent_mid[0, j], tops), 1.0, 0.0)

    loads[0].wait()
    loads[1].wait()
    for k in range(leaves):
        xl[k] = live_rows(dot(il[k], rl[k]), 0, width_leaf[0, k]).astype(BF16)
    store_leaf = pltpu.make_async_copy(xl, leaf_out.at[0], store_sems.at[0])
    store_leaf.start()

    for load in loads[2:5]:
        load.wait()
    for j in range(mids):
        total = dot(
            jnp.concatenate([lm[first[j]], lm[last[j]]], axis=1),
            jnp.concatenate([xl[first[j]], xl[last[j]]], axis=0),
        )
        mid_input = (rm[j].astype(F32) - total).astype(BF16)
        xm[j] = live_rows(dot(im[j], mid_input), 0, width_mid[0, j]).astype(BF16)
    store_mid = pltpu.make_async_copy(xm, mid_out.at[0], store_sems.at[1])
    store_mid.start()
    for load in loads[7:]:
        load.start()

    pl.semaphore_wait(barrier, len(partners))
    mask_copy = remote(mask, mask_rx, core_s.at[0], core_r.at[0], (z, sibling, y))
    mask_copy.start()

    slot = lax.rem(pc, nx)
    target_core = pc // nx
    pre_copies = []
    for d in range(nx):
        tx = lax.rem(x + d, nx)
        s = y * per_y + tx // half
        column = pl.multiple_of(lax.rem(tx, half) * LANES, LANES)
        pairs = (
            (inv_top.at[s], inv.at[slot]),
            (rhs_top.at[s, :, pl.ds(column, LANES)], rhs.at[slot]),
        )
        for i, (src, dst) in enumerate(pairs):
            copy = remote(
                src, dst, pre_s.at[i, d], pre_r.at[i, slot], (z, 2 * tx + target_core, y)
            )
            pre_copies.append((d, copy))
            if d == 0:
                @pl.when(target_core == c)
                def _():
                    pltpu.make_async_copy(src, dst, pre_r.at[i, slot]).start()

                @pl.when(target_core != c)
                def _():
                    copy.start()
            else:
                copy.start()

    loads[5].wait()
    loads[6].wait()
    for j in range(mids):
        low, high = first[j], last[j]
        xu[j] = jnp.concatenate([
            xm[j], flagged(xl[low], pattern_leaf[0, low]), flagged(xl[high], pattern_leaf[0, high])
        ], axis=0)
    up_copies = []
    for q_ in range(chunks):
        for j in range(mids):
            low, high = first[j], last[j]
            spans = [
                pl.ds(core * half_rows + q_ * block_rows, block_rows) for core in range(2)
            ]
            update = dot(
                jnp.concatenate([
                    jnp.concatenate([mt[j, span, :], lt[low, span, :], lt[high, span, :]], axis=1)
                    for span in spans
                ], axis=0),
                xu[j],
            )
            up_own[q_, j] = update.reshape(2, block_rows, num_rhs).astype(BF16)
            i = 1 + q_ * mids + j
            up_copies.append(remote(
                up_own.at[q_, j, other], up_rx.at[q_, j], core_s.at[i], core_r.at[i],
                (z, sibling, y),
            ))
            up_copies[-1].start()
    last_sem = 1 + chunks * mids
    w_copy = remote(
        off_top_out.at[:, :, pl.ds(pl.multiple_of(other * half_rows, half_rows), half_rows)],
        wt.at[:, c], core_s.at[last_sem], core_r.at[last_sem], (z, sibling, y),
    )

    mask_copy.wait_recv()
    step = 16
    far_x = sorted(range(1, nx), key=lambda d: -min(d, nx - d))
    far_y = sorted(range(1, ny), key=lambda d: -min(d, ny - d))
    a_copies, b_copies = [], []
    for q_ in range(chunks):
        for copy in up_copies[q_ * mids:(q_ + 1) * mids]:
            copy.wait_recv()
        for p in range(2):
            def pair_sum(i, carry):
                at = pl.multiple_of(i * step, step)
                span = pl.ds(pl.multiple_of(p * part + at, step), step)
                blocks = [up_own[q_, j, c, span, :].astype(F32) for j in range(mids)]
                blocks += [up_rx[q_, j, span, :].astype(F32) for j in range(mids)]
                for s in range(tops):
                    for h in range(half):
                        total = jnp.zeros((step, LANES), F32)
                        for j in range(2 * mids):
                            table = mask if j < mids else mask_rx
                            weight = table[j % mids, s:s + 1, :]
                            total += weight * blocks[j][:, h * LANES:(h + 1) * LANES]
                        t_sum[q_, p, s // per_y, (s % per_y) * half + h, pl.ds(at, step), :] = (
                            total.astype(BF16)
                        )
                return carry

            lax.fori_loop(0, part // step, pair_sum, 0)
            if p == 0:
                a_copies.append([])
                for d in far_x:
                    tx = lax.rem(x + d, nx)
                    a_copies[q_].append(remote(
                        t_sum.at[q_, 0, :, tx], a_rx.at[q_, d - 1],
                        a_s.at[q_, d - 1], a_r.at[q_, d - 1], (z, 2 * tx + c, y),
                    ))
                    a_copies[q_][-1].start()
            else:
                b_copies.append([])
                for d in far_y:
                    ty = lax.rem(y + d, ny)
                    b_copies[q_].append(remote(
                        t_sum.at[q_, 1, ty], b_rx.at[q_, d - 1],
                        b_s.at[q_, d - 1], b_r.at[q_, d - 1], (z, pc, ty),
                    ))
                    b_copies[q_][-1].start()
    w_copy.start()

    leaf_w, mid_w = xl.shape[1], xm.shape[1]
    for k in range(leaves):
        xo[k * leaf_w:(k + 1) * leaf_w] = flagged(xl[k], pattern_leaf[1, k])
    base = leaves * leaf_w
    for j in range(mids):
        xo[base + j * mid_w:base + (j + 1) * mid_w] = flagged(xm[j], pattern_mid[0, j])
    loads[7].wait()
    loads[8].wait()

    def outer_rows(i, carry):
        block = pl.ds(pl.multiple_of(i * 2 * rows, 2 * rows), 2 * rows)
        total = dot(
            jnp.concatenate(
                [ol[k, block, :] for k in range(leaves)] + [om[j, block, :] for j in range(mids)],
                axis=1,
            ),
            xo[...],
        )
        for core in range(2):
            across = total[core * rows:(core + 1) * rows].T
            o_t[core, i] = across.reshape(nz, wide, rows).astype(BF16)
        return carry

    lax.fori_loop(0, nx, outer_rows, 0)
    o_core = remote(
        o_t.at[other], o_rx, core_s.at[last_sem + 1], core_r.at[last_sem + 1], (z, sibling, y)
    )
    o_core.start()

    a2_copies, b2_copies = [], []
    for q_ in range(chunks):
        for copy in a_copies[q_]:
            copy.wait_recv()
        for i in range(ny):
            total = t_sum[q_, 0, i, x].astype(F32)
            for d in range(nx - 1):
                total += a_rx[q_, d, i].astype(F32)
            a_sum[q_, i] = total.astype(BF16)
        a2_copies.append([])
        for d in far_y:
            ty = lax.rem(y + d, ny)
            a2_copies[q_].append(remote(
                a_sum.at[q_, ty], a_rx2.at[q_, d - 1],
                a2_s.at[q_, d - 1], a2_r.at[q_, d - 1], (z, pc, ty),
            ))
            a2_copies[q_][-1].start()
        for copy in b_copies[q_]:
            copy.wait_recv()
        for i in range(nx):
            total = t_sum[q_, 1, y, i].astype(F32)
            for d in range(ny - 1):
                total += b_rx[q_, d, i].astype(F32)
            b_sum[q_, i] = total.astype(BF16)
        b2_copies.append([])
        for d in far_x:
            tx = lax.rem(x + d, nx)
            b2_copies[q_].append(remote(
                b_sum.at[q_, tx], b_rx2.at[q_, d - 1],
                b2_s.at[q_, d - 1], b2_r.at[q_, d - 1], (z, 2 * tx + c, y),
            ))
            b2_copies[q_][-1].start()
        if q_ == 0:
            o_core.wait_recv()
            oz_copies = []

            def outer_pair(i, carry):
                o_s[i] = (o_t[c, i].astype(F32) + o_rx[i].astype(F32)).astype(BF16)
                return carry

            lax.fori_loop(0, nx, outer_pair, 0)
            for d in range(1, nz):
                tz = lax.rem(z + d, nz)
                oz_copies.append(remote(
                    o_s.at[:, tz], o_rz.at[d - 1], oz_s.at[d - 1], oz_r.at[d - 1], (tz, pc, y),
                ))
                oz_copies[-1].start()

    for i in range(nx):
        pre = [
            remote(inv_top.at[0], inv.at[i], pre_s.at[0, 0], pre_r.at[0, i], (z, sibling, y)),
            remote(rhs_top.at[0, :, pl.ds(0, LANES)], rhs.at[i], pre_s.at[1, 0], pre_r.at[1, i],
                   (z, sibling, y)),
        ]
        for copy in pre:
            copy.wait_recv()
    right = rhs[...].reshape(chunks, 2, part, LANES).astype(F32)
    in_copies = []
    for q_ in range(chunks):
        for copy in a2_copies[q_]:
            copy.wait_recv()
        total = a_sum[q_, y].astype(F32)
        for d in range(ny - 1):
            total += a_rx2[q_, d].astype(F32)
        top_in[c, q_, pl.ds(0, part), :] = (right[q_, 0] - total).astype(BF16)
        for copy in b2_copies[q_]:
            copy.wait_recv()
        total = b_sum[q_, x].astype(F32)
        for d in range(nx - 1):
            total += b_rx2[q_, d].astype(F32)
        top_in[c, q_, pl.ds(part, part), :] = (right[q_, 1] - total).astype(BF16)
        i = last_sem + 2 + q_
        in_copies.append(remote(
            top_in.at[c, q_], top_in.at[c, q_], core_s.at[i], core_r.at[i], (z, sibling, y)
        ))
        in_copies[-1].start()
    for copy in in_copies:
        copy.wait_recv()

    block = dot(inv[...].reshape(half_rows, inv.shape[2]), top_in[...].reshape(2 * half_rows, LANES))
    block = live_rows(block, c * half_rows, width_top[y * per_y + x // half])
    across = block.T.reshape(nz // half, ny, chunk, half_rows)
    for i in range(ny):
        turned[i] = across[:, i].reshape(group, half_rows).astype(BF16)
    unit[...] = block.reshape(nx, slab, LANES).astype(BF16)

    g_copies = []
    steps = [(dx, dy) for dy in range(ny) for dx in range(nx) if dx or dy]
    for dx, dy in sorted(steps, key=lambda d: -min(d[0], nx - d[0]) - min(d[1], ny - d[1])):
        tx = lax.rem(x + dx, nx)
        ty = lax.rem(y + dy, ny)
        i = dy * nx + dx - 1
        g_copies.append(remote(
            turned.at[ty], gathered.at[y, x], g_s.at[i], g_r.at[i], (z, 2 * tx + c, ty),
        ))
        g_copies[-1].start()
    gathered[y, x] = turned[y]

    sol_copies = []
    for d in range(nx):
        i = lax.rem(slot + d, nx)
        copy = remote(
            unit.at[i], sol_rx.at[x], sol_s.at[d], sol_r.at[x], (z, nx * c + i, y)
        )
        sol_copies.append((d, copy))
        if d == 0:
            @pl.when(target_core == c)
            def _():
                pltpu.make_async_copy(unit.at[i], sol_rx.at[x], sol_r.at[x]).start()

            @pl.when(target_core != c)
            def _():
                copy.start()
        else:
            copy.start()

    for copy in oz_copies:
        copy.wait_recv()
    ox_copies = []
    for i in range(nx):
        total = o_s[i, z].astype(F32)
        for d in range(nz - 1):
            total += o_rz[d, i].astype(F32)
        o_z[i] = total.astype(BF16)
    for d in range(1, nx):
        tx = lax.rem(x + d, nx)
        ox_copies.append(remote(
            o_z.at[tx], o_rx2.at[d - 1], ox_s.at[d - 1], ox_r.at[d - 1], (z, 2 * tx + c, y),
        ))
        ox_copies[-1].start()

    loads[9].wait()
    w_copy.wait_recv()
    for copy in g_copies:
        copy.wait_recv()

    total = jnp.zeros((half * group, 2 * rows), F32)
    for i in range(ny):
        for t in range(per_y):
            left = gathered[i, t * half:(t + 1) * half].reshape(half * group, half_rows)
            total += dot_nt(left, wt[i * per_y + t].reshape(2 * rows, half_rows))
    for core in range(2):
        q[core] = total[:, core * rows:(core + 1) * rows].reshape(nz, chunk, rows)
    q_copies = []
    steps = [(dz, dc) for dz in range(nz) for dc in range(2) if dz or dc]
    for dz, dc in sorted(steps, key=lambda d: -min(d[0], nz - d[0])):
        tz = lax.rem(z + dz, nz)
        tc = lax.rem(c + dc, 2)
        i = 2 * dz + dc - 1
        q_copies.append(remote(
            q.at[tc, tz], terms_out.at[i], q_s.at[i], q_r.at[i], (tz, 2 * x + tc, y),
        ))
        q_copies[-1].start()

    for copy in ox_copies:
        copy.wait_recv()
    total = o_z[x].astype(F32)
    for d in range(nx - 1):
        total += o_rx2[d].astype(F32)
    o_x[...] = total.reshape(ny, chunk, rows)
    oy_copies = []
    for d in range(1, ny):
        ty = lax.rem(y + d, ny)
        oy_copies.append(remote(
            o_x.at[ty], o_ry.at[d - 1], oy_s.at[d - 1], oy_r.at[d - 1], (z, pc, ty),
        ))
        oy_copies[-1].start()
    for i in range(nx):
        remote(unit.at[0], sol_rx.at[i], sol_s.at[0], sol_r.at[i], (z, sibling, y)).wait_recv()
    for t in range(per_y):
        for h in range(half):
            sol_v[t, :, h * LANES:(h + 1) * LANES] = sol_rx[t * half + h]
    store_sol = pltpu.make_async_copy(sol_v, top_solution, store_sems.at[2])
    store_sol.start()
    for copy in oy_copies:
        copy.wait_recv()
    total = o_x[y]
    for d in range(ny - 1):
        total += o_ry[d]
    own_v[...] = total + q[c, z]
    store_own = pltpu.make_async_copy(own_v, terms_out.at[2 * nz - 1], store_sems.at[3])
    store_own.start()

    for copy in (
        [mask_copy, w_copy, o_core] + in_copies + up_copies
        + sum(a_copies + b_copies + a2_copies + b2_copies, [])
        + g_copies + oz_copies + ox_copies + oy_copies
    ):
        copy.wait_send()
    for d, copy in pre_copies + sol_copies:
        if d == 0:
            @pl.when(target_core != c)
            def _():
                copy.wait_send()
        else:
            copy.wait_send()
    store_leaf.wait()
    store_mid.wait()
    store_sol.wait()
    store_own.wait()
    for copy in q_copies:
        copy.wait_recv()
    for copy in q_copies:
        copy.wait_send()


def finish_kernel(*refs):
    count = (len(refs) - 3) // 3
    ins, outs, held = refs[:count], refs[count:2 * count], refs[2 * count:3 * count]
    outer_v, in_sems, out_sems = refs[-3:]
    loads = [pltpu.make_async_copy(ins[i], held[i], in_sems.at[i]) for i in range(count)]
    for load in loads:
        load.start()
    stores = []
    for i in range(count):
        loads[i].wait()
        if i == count - 1:
            total = held[i][0]
            for d in range(1, held[i].shape[0]):
                total += held[i][d]
            outer_v[...] = total
        source = outer_v if i == count - 1 else held[i]
        stores.append(pltpu.make_async_copy(source, outs[i], out_sems.at[i]))
        stores[-1].start()
    for store in stores:
        store.wait()


def on_device(
    nz, nx, ny,
    rhs_leaf, rhs_mid, rhs_top, inv_leaf, inv_mid, inv_top,
    off_leaf_mid, off_leaf_top, off_leaf_out, off_mid_top, off_mid_out, off_top_out,
    parent_leaf, parent_mid, width_leaf, width_mid, width_top, pattern_leaf, pattern_mid,
):
    hbm = pl.BlockSpec(memory_space=pl.ANY)
    leaves, leaf_w, num_rhs = rhs_leaf.shape[1:]
    mids, mid_w = rhs_mid.shape[1:3]
    tops, slab = rhs_top.shape[:2]
    top_w = inv_top.shape[2]
    outer = off_leaf_out.shape[2]
    rows = off_top_out.shape[1]
    half = num_rhs // LANES
    per_y = tops // ny
    assert per_y * half == nx and slab * 2 * nx == top_w and rows * 2 * nx == outer
    half_rows = top_w // 2
    chunks = CHUNKS
    part = half_rows // chunks // 2
    wide = num_rhs // nz
    chunk = wide // ny
    group = nz // half * chunk

    def vm(*shape, dtype=BF16):
        return pltpu.VMEM(shape, dtype)

    sems = pltpu.SemaphoreType.DMA
    results = pl.pallas_call(
        functools.partial(window_kernel, nz, nx, ny),
        out_shape=(
            jax.ShapeDtypeStruct(rhs_leaf.shape, BF16),
            jax.ShapeDtypeStruct(rhs_mid.shape, BF16),
            jax.ShapeDtypeStruct((per_y, slab, num_rhs), BF16),
            jax.ShapeDtypeStruct((2 * nz, chunk, rows), F32),
        ),
        in_specs=[hbm] * 19,
        out_specs=(hbm,) * 4,
        scratch_shapes=[
            pltpu.SMEM((1, leaves), jnp.int32), pltpu.SMEM((1, mids), jnp.int32),
            pltpu.SMEM((1, leaves), jnp.int32), pltpu.SMEM((1, mids), jnp.int32),
            pltpu.SMEM((tops,), jnp.int32), pltpu.SMEM((2, leaves), jnp.int32),
            pltpu.SMEM((1, mids), jnp.int32),
            vm(leaves, leaf_w, num_rhs), vm(leaves, leaf_w, leaf_w), vm(leaves, mid_w, leaf_w),
            vm(mids, mid_w, num_rhs), vm(mids, mid_w, mid_w),
            vm(leaves, top_w, leaf_w), vm(mids, top_w, mid_w),
            vm(leaves, leaf_w, num_rhs), vm(mids, mid_w, num_rhs),
            vm(leaves, outer, leaf_w), vm(mids, outer, mid_w),
            vm(leaves * leaf_w + mids * mid_w, num_rhs),
            vm(mids, mid_w + 2 * leaf_w, num_rhs),
            vm(chunks, mids, 2, 2 * part, num_rhs), vm(chunks, mids, 2 * part, num_rhs),
            vm(mids, max(tops, 8), LANES, dtype=F32), vm(mids, max(tops, 8), LANES, dtype=F32),
            vm(chunks, 2, ny, nx, part, LANES),
            vm(chunks, nx - 1, ny, part, LANES), vm(chunks, ny - 1, nx, part, LANES),
            vm(chunks, ny, part, LANES), vm(chunks, nx, part, LANES),
            vm(chunks, ny - 1, part, LANES), vm(chunks, nx - 1, part, LANES),
            vm(2, chunks, 2 * part, LANES), vm(nx, slab, top_w), vm(nx, slab, LANES),
            vm(nx, slab, LANES), vm(nx, slab, LANES), vm(per_y, slab, num_rhs),
            vm(ny, group, half_rows), vm(ny, nx, group, half_rows),
            vm(tops, 2, rows, half_rows),
            vm(2, nx, nz, wide, rows), vm(nx, nz, wide, rows), vm(nx, nz, wide, rows),
            vm(nz - 1, nx, wide, rows), vm(nx, wide, rows), vm(nx - 1, wide, rows),
            vm(ny, chunk, rows, dtype=F32), vm(ny - 1, chunk, rows, dtype=F32),
            vm(2, nz, chunk, rows, dtype=F32), vm(chunk, rows, dtype=F32),
            sems((7,)), sems((10,)), sems((4,)),
            sems((3 + chunks * (mids + 1),)), sems((3 + chunks * (mids + 1),)),
            sems((2, nx)), sems((2, nx)),
            sems((chunks, nx - 1)), sems((chunks, nx - 1)),
            sems((chunks, ny - 1)), sems((chunks, ny - 1)),
            sems((chunks, ny - 1)), sems((chunks, ny - 1)),
            sems((chunks, nx - 1)), sems((chunks, nx - 1)),
            sems((nx,)), sems((nx,)), sems((nx * ny - 1,)), sems((nx * ny - 1,)),
            sems((nz - 1,)), sems((nz - 1,)), sems((nx - 1,)), sems((nx - 1,)),
            sems((ny - 1,)), sems((ny - 1,)), sems((2 * nz - 1,)), sems((2 * nz - 1,)),
        ],
        compiler_params=pltpu.CompilerParams(
            collective_id=0, has_side_effects=True, vmem_limit_bytes=60 << 20
        ),
        name="window",
    )(
        parent_leaf.reshape(1, leaves), parent_mid.reshape(1, mids), width_leaf, width_mid,
        width_top, jnp.transpose(pattern_leaf[0], (1, 0)), pattern_mid,
        rhs_leaf, rhs_mid, rhs_top, inv_leaf, inv_mid, inv_top,
        off_leaf_mid, off_leaf_top, off_leaf_out, off_mid_top, off_mid_out, off_top_out,
    )
    shapes = [jax.ShapeDtypeStruct(a.shape, a.dtype) for a in results[:3]]
    shapes.append(jax.ShapeDtypeStruct((chunk, rows), F32))
    leaf_x, mid_x, top_solution, outer_part = pl.pallas_call(
        finish_kernel,
        out_shape=tuple(shapes),
        in_specs=[hbm] * 4,
        out_specs=(hbm,) * 4,
        scratch_shapes=[vm(*a.shape, dtype=a.dtype) for a in results]
        + [vm(chunk, rows, dtype=F32), sems((4,)), sems((4,))],
        compiler_params=pltpu.CompilerParams(vmem_limit_bytes=60 << 20),
        name="finish",
    )(*results)
    return leaf_x, mid_x, top_solution, outer_part.T


def solution(mesh):
    sizes = dict(mesh.shape)
    deep = P("gz", ("pr", "pc"), None, None)
    flat = P("pr", "pc", None)
    return jax.shard_map(
        functools.partial(on_device, sizes["pr"], sizes["pc"] // 2, sizes["gz"]),
        mesh=mesh,
        in_specs=(
            deep, deep, flat, deep, deep, flat,
            deep, deep, deep, deep, deep, flat,
            P("gz", ("pr", "pc"), None),
            P("gz", ("pr", "pc"), None),
            P("gz", ("pr", "pc")),
            P("gz", ("pr", "pc")),
            P("pr"),
            P("gz", ("pr", "pc"), None),
            P("gz", ("pr", "pc")),
        ),
        out_specs=(deep, deep, P(("pr", "gz"), "pc", None), P("pc", ("pr", "gz"))),
        check_vma=False,
    )
```

time: 45.5 us -> 43.1 us (0.947)
  Pallas kernels: 44.7 us -> 42.3 us
    pallas_call x1, Pallas kernels: 42.7 us -> 40.2 us  [on_device(): pl.pallas_call(functools.partial(window_kernel, nz, nx, ny), out_shape=(j...]
where the time goes in v3:
time: 43.1 us; the launch traced here: 43 us
  Pallas kernels  42.3 us (98%)
  between operations  0.65 us (2%)
    pallas_call x1, Pallas kernels, on_device(): pl.pallas_call(functools.partial(window_kernel, nz, nx, ny), out_shape=(j...  40.2 us
    pallas_call x1, Pallas kernels, on_device(): pl.pallas_call(finish_kernel, out_shape=tuple(shapes), in_specs=[hbm] * 4...  2.09 us

profile of v3, /device:TPU:1, one launch (start us, length us, event | category | flops | bytes accessed | tf_op | source)
XLA Modules:
  0.0 43.0 jit_solution(9167607914058560519)
XLA Ops:
  0.6 40.2 %window.1 = (bf16[1,8,128,256]{3,2,1,0:T(8,128)(2,1)}, bf16[1,4,256,256]{3,2,1,0:T(8,128)(2,1)}, bf16[2,64,256]{2,1,0:T(8,128)(2,1)}, f32[16,8,128]{2,1,0:T(8,128)}) custom-call(s32[1,8]{1,0:T(1,128)} %bitcast.7, s32[1,4]{1,0:T(1,128)} %bitcast.8, s32[1,8]{1,0:T(1,128)} %width_leaf_in.1, s32[1,4]{1,0:T(1,128)} %width_mid_in.1, s32[8]{0:T(128)} %width_top_in.1, ...), custom_call_target="tpu_custom_call" | custom-call | tf_op jit(solution)/shard_map/window/pallas_call | solution.py:541
  40.9 2.1 %finish.1 = (bf16[1,8,128,256]{3,2,1,0:T(8,128)(2,1)}, bf16[1,4,256,256]{3,2,1,0:T(8,128)(2,1)}, bf16[2,64,256]{2,1,0:T(8,128)(2,1)}, f32[8,128]{1,0:T(8,128)}) custom-call(bf16[1,8,128,256]{3,2,1,0:T(8,128)(2,1)} %get-tuple-element.12.refs_0_, bf16[1,4,256,256]{3,2,1,0:T(8,128)(2,1)} %get-tuple-element.13.refs_1_, ...), custom_call_target="tpu_custom_call" | custom-call | tf_op jit(solution)/shard_map/finish/pallas_call | solution.py:600

commit v4 on v3

--- a/solution.py
+++ b/solution.py
@@ -39,11 +39,11 @@
     off_leaf_mid, off_leaf_top, off_leaf_out, off_mid_top, off_mid_out, off_top_out,
     leaf_out, mid_out, top_solution, terms_out,
     parent_leaf, parent_mid, width_leaf, width_mid, width_top, pattern_leaf, pattern_mid,
-    rl, il, lm, rm, im, lt, mt, xl, xm, ol, om, xo, xu, up_own, up_rx, mask, mask_rx,
+    rl, il, lm, rm, im, lt, mt, ol, om, xo, xu, up_own, up_rx, mask, mask_rx,
     t_sum, a_rx, b_rx, a_sum, b_sum, a_rx2, b_rx2, top_in, inv, rhs,
-    unit, sol_rx, sol_v, turned, gathered, wt,
-    o_t, o_rx, o_s, o_rz, o_z, o_rx2, o_x, o_ry, q, own_v,
-    vector_sems, load_sems, store_sems, core_s, core_r, pre_s, pre_r, a_s, a_r, b_s, b_r, a2_s, a2_r, b2_s, b2_r,
+    unit, sol_rx, turned, gathered, wt,
+    o_t, o_rx, o_s, o_rz, o_z, o_rx2, o_x, o_ry, q,
+    vector_sems, load_sems, core_s, core_r, pre_s, pre_r, a_s, a_r, b_s, b_r, a2_s, a2_r, b2_s, b2_r,
     sol_s, sol_r, g_s, g_r, oz_s, oz_r, ox_s, ox_r, oy_s, oy_r, q_s, q_r,
 ):
     z = lax.axis_index("pr")
@@ -53,6 +53,7 @@
     c = pc % 2
     other = 1 - c
     sibling = 2 * x + other
+    xl, xm = leaf_out.at[0], mid_out.at[0]
     leaves, mids = xl.shape[0], xm.shape[0]
     tops = rhs_top.shape[0]
     per_y = tops // ny
@@ -90,19 +91,23 @@
     loads = [
         pltpu.make_async_copy(src, dst, load_sems.at[i]) for i, (src, dst) in enumerate(load_pairs)
     ]
-    for load in loads[:2] + vectors + loads[2:7]:
+    for load in loads[:2] + vectors[:4] + loads[2:5]:
         load.start()
 
     barrier = pltpu.get_barrier_semaphore()
-    partners = [(z, lax.rem(pc + d, 2 * nx), y) for d in range(1, 2 * nx)]
-    for dy in range(1, ny):
-        for dx in range(nx):
-            partners.append((z, lax.rem(pc + 2 * dx, 2 * nx), lax.rem(y + dy, ny)))
-    for dz in range(1, nz):
+    partners = []
+    for d in sorted(range(1, nz), key=lambda d: -min(d, nz - d)):
         for core in range(2):
-            partners.append((lax.rem(z + dz, nz), 2 * x + core, y))
+            partners.append((lax.rem(z + d, nz), 2 * x + core, y))
+    steps = [(dx, dy) for dy in range(ny) for dx in range(nx) if dx or dy]
+    for dx, dy in sorted(steps, key=lambda d: -min(d[0], nx - d[0]) - min(d[1], ny - d[1])):
+        partners.append((z, 2 * lax.rem(x + dx, nx) + c, lax.rem(y + dy, ny)))
+    for dx in range(nx):
+        partners.append((z, 2 * lax.rem(x + dx, nx) + other, y))
     for partner in partners:
         pl.semaphore_signal(barrier, inc=1, device_id=partner, device_id_type=MESH_IDS)
+    for load in loads[5:7] + vectors[4:]:
+        load.start()
     for vector in vectors:
         vector.wait()
 
@@ -125,8 +130,6 @@
     loads[1].wait()
     for k in range(leaves):
         xl[k] = live_rows(dot(il[k], rl[k]), 0, width_leaf[0, k]).astype(BF16)
-    store_leaf = pltpu.make_async_copy(xl, leaf_out.at[0], store_sems.at[0])
-    store_leaf.start()
 
     for load in loads[2:5]:
         load.wait()
@@ -137,41 +140,8 @@
         )
         mid_input = (rm[j].astype(F32) - total).astype(BF16)
         xm[j] = live_rows(dot(im[j], mid_input), 0, width_mid[0, j]).astype(BF16)
-    store_mid = pltpu.make_async_copy(xm, mid_out.at[0], store_sems.at[1])
-    store_mid.start()
     for load in loads[7:]:
         load.start()
-
-    pl.semaphore_wait(barrier, len(partners))
-    mask_copy = remote(mask, mask_rx, core_s.at[0], core_r.at[0], (z, sibling, y))
-    mask_copy.start()
-
-    slot = lax.rem(pc, nx)
-    target_core = pc // nx
-    pre_copies = []
-    for d in range(nx):
-        tx = lax.rem(x + d, nx)
-        s = y * per_y + tx // half
-        column = pl.multiple_of(lax.rem(tx, half) * LANES, LANES)
-        pairs = (
-            (inv_top.at[s], inv.at[slot]),
-            (rhs_top.at[s, :, pl.ds(column, LANES)], rhs.at[slot]),
-        )
-        for i, (src, dst) in enumerate(pairs):
-            copy = remote(
-                src, dst, pre_s.at[i, d], pre_r.at[i, slot], (z, 2 * tx + target_core, y)
-            )
-            pre_copies.append((d, copy))
-            if d == 0:
-                @pl.when(target_core == c)
-                def _():
-                    pltpu.make_async_copy(src, dst, pre_r.at[i, slot]).start()
-
-                @pl.when(target_core != c)
-                def _():
-                    copy.start()
-            else:
-                copy.start()
 
     loads[5].wait()
     loads[6].wait()
@@ -194,14 +164,17 @@
                 ], axis=0),
                 xu[j],
             )
-            up_own[q_, j] = update.reshape(2, block_rows, num_rhs).astype(BF16)
-            i = 1 + q_ * mids + j
-            up_copies.append(remote(
-                up_own.at[q_, j, other], up_rx.at[q_, j], core_s.at[i], core_r.at[i],
-                (z, sibling, y),
-            ))
-            up_copies[-1].start()
-    last_sem = 1 + chunks * mids
+            for core in range(2):
+                up_own[q_, core, j] = update[core * block_rows:(core + 1) * block_rows].astype(BF16)
+        if q_ == 0:
+            pl.semaphore_wait(barrier, len(partners))
+            mask_copy = remote(mask, mask_rx, core_s.at[0], core_r.at[0], (z, sibling, y))
+            mask_copy.start()
+        up_copies.append(remote(
+            up_own.at[q_, other], up_rx.at[q_], core_s.at[1 + q_], core_r.at[1 + q_], (z, sibling, y)
+        ))
+        up_copies[-1].start()
+    last_sem = 1 + chunks
     w_copy = remote(
         off_top_out.at[:, :, pl.ds(pl.multiple_of(other * half_rows, half_rows), half_rows)],
         wt.at[:, c], core_s.at[last_sem], core_r.at[last_sem], (z, sibling, y),
@@ -213,13 +186,12 @@
     far_y = sorted(range(1, ny), key=lambda d: -min(d, ny - d))
     a_copies, b_copies = [], []
     for q_ in range(chunks):
-        for copy in up_copies[q_ * mids:(q_ + 1) * mids]:
-            copy.wait_recv()
+        up_copies[q_].wait_recv()
         for p in range(2):
             def pair_sum(i, carry):
                 at = pl.multiple_of(i * step, step)
                 span = pl.ds(pl.multiple_of(p * part + at, step), step)
-                blocks = [up_own[q_, j, c, span, :].astype(F32) for j in range(mids)]
+                blocks = [up_own[q_, c, j, span, :].astype(F32) for j in range(mids)]
                 blocks += [up_rx[q_, j, span, :].astype(F32) for j in range(mids)]
                 for s in range(tops):
                     for h in range(half):
@@ -252,6 +224,33 @@
                         b_s.at[q_, d - 1], b_r.at[q_, d - 1], (z, pc, ty),
                     ))
                     b_copies[q_][-1].start()
+    slot = lax.rem(pc, nx)
+    target_core = pc // nx
+    pre_copies = []
+    for d in range(nx):
+        tx = lax.rem(x + d, nx)
+        s = y * per_y + tx // half
+        column = pl.multiple_of(lax.rem(tx, half) * LANES, LANES)
+        pairs = (
+            (inv_top.at[s], inv.at[slot]),
+            (rhs_top.at[s, :, pl.ds(column, LANES)], rhs.at[slot]),
+        )
+        for i, (src, dst) in enumerate(pairs):
+            copy = remote(
+                src, dst, pre_s.at[i, d], pre_r.at[i, slot], (z, 2 * tx + target_core, y)
+            )
+            pre_copies.append((d, copy))
+            if d == 0:
+                @pl.when(target_core == c)
+                def _():
+                    pltpu.make_async_copy(src, dst, pre_r.at[i, slot]).start()
+
+                @pl.when(target_core != c)
+                def _():
+                    copy.start()
+            else:
+                copy.start()
+
     w_copy.start()
 
     leaf_w, mid_w = xl.shape[1], xm.shape[1]
@@ -454,17 +453,13 @@
         remote(unit.at[0], sol_rx.at[i], sol_s.at[0], sol_r.at[i], (z, sibling, y)).wait_recv()
     for t in range(per_y):
         for h in range(half):
-            sol_v[t, :, h * LANES:(h + 1) * LANES] = sol_rx[t * half + h]
-    store_sol = pltpu.make_async_copy(sol_v, top_solution, store_sems.at[2])
-    store_sol.start()
+            top_solution[t, :, h * LANES:(h + 1) * LANES] = sol_rx[t * half + h]
     for copy in oy_copies:
         copy.wait_recv()
     total = o_x[y]
     for d in range(ny - 1):
         total += o_ry[d]
-    own_v[...] = total + q[c, z]
-    store_own = pltpu.make_async_copy(own_v, terms_out.at[2 * nz - 1], store_sems.at[3])
-    store_own.start()
+    terms_out[2 * nz - 1] = total + q[c, z]
 
     for copy in (
         [mask_copy, w_copy, o_core] + in_copies + up_copies
@@ -479,34 +474,26 @@
                 copy.wait_send()
         else:
             copy.wait_send()
-    store_leaf.wait()
-    store_mid.wait()
-    store_sol.wait()
-    store_own.wait()
     for copy in q_copies:
         copy.wait_recv()
     for copy in q_copies:
         copy.wait_send()
 
 
-def finish_kernel(*refs):
-    count = (len(refs) - 3) // 3
-    ins, outs, held = refs[:count], refs[count:2 * count], refs[2 * count:3 * count]
-    outer_v, in_sems, out_sems = refs[-3:]
-    loads = [pltpu.make_async_copy(ins[i], held[i], in_sems.at[i]) for i in range(count)]
-    for load in loads:
-        load.start()
-    stores = []
-    for i in range(count):
-        loads[i].wait()
-        if i == count - 1:
-            total = held[i][0]
-            for d in range(1, held[i].shape[0]):
-                total += held[i][d]
-            outer_v[...] = total
-        source = outer_v if i == count - 1 else held[i]
-        stores.append(pltpu.make_async_copy(source, outs[i], out_sems.at[i]))
-        stores[-1].start()
+def finish_kernel(
+    leaf_x, mid_x, solved, terms, leaf_out, mid_out, top_solution, outer_out, outer_v, out_sems
+):
+    pairs = ((leaf_x, leaf_out), (mid_x, mid_out), (solved, top_solution), (outer_v, outer_out))
+    stores = [
+        pltpu.make_async_copy(src, dst, out_sems.at[i]) for i, (src, dst) in enumerate(pairs)
+    ]
+    for store in stores[:3]:
+        store.start()
+    total = terms[0]
+    for d in range(1, terms.shape[0]):
+        total += terms[d]
+    outer_v[...] = total
+    stores[3].start()
     for store in stores:
         store.wait()
 
@@ -518,6 +505,7 @@
     parent_leaf, parent_mid, width_leaf, width_mid, width_top, pattern_leaf, pattern_mid,
 ):
     hbm = pl.BlockSpec(memory_space=pl.ANY)
+    vmem = pl.BlockSpec(memory_space=pltpu.VMEM)
     leaves, leaf_w, num_rhs = rhs_leaf.shape[1:]
     mids, mid_w = rhs_mid.shape[1:3]
     tops, slab = rhs_top.shape[:2]
@@ -541,13 +529,13 @@
     results = pl.pallas_call(
         functools.partial(window_kernel, nz, nx, ny),
         out_shape=(
-            jax.ShapeDtypeStruct(rhs_leaf.shape, BF16),
-            jax.ShapeDtypeStruct(rhs_mid.shape, BF16),
-            jax.ShapeDtypeStruct((per_y, slab, num_rhs), BF16),
-            jax.ShapeDtypeStruct((2 * nz, chunk, rows), F32),
+            pltpu.VMEM(rhs_leaf.shape, BF16),
+            pltpu.VMEM(rhs_mid.shape, BF16),
+            pltpu.VMEM((per_y, slab, num_rhs), BF16),
+            pltpu.VMEM((2 * nz, chunk, rows), F32),
         ),
         in_specs=[hbm] * 19,
-        out_specs=(hbm,) * 4,
+        out_specs=(vmem,) * 4,
         scratch_shapes=[
             pltpu.SMEM((1, leaves), jnp.int32), pltpu.SMEM((1, mids), jnp.int32),
             pltpu.SMEM((1, leaves), jnp.int32), pltpu.SMEM((1, mids), jnp.int32),
@@ -556,26 +544,25 @@
             vm(leaves, leaf_w, num_rhs), vm(leaves, leaf_w, leaf_w), vm(leaves, mid_w, leaf_w),
             vm(mids, mid_w, num_rhs), vm(mids, mid_w, mid_w),
             vm(leaves, top_w, leaf_w), vm(mids, top_w, mid_w),
-            vm(leaves, leaf_w, num_rhs), vm(mids, mid_w, num_rhs),
             vm(leaves, outer, leaf_w), vm(mids, outer, mid_w),
             vm(leaves * leaf_w + mids * mid_w, num_rhs),
             vm(mids, mid_w + 2 * leaf_w, num_rhs),
-            vm(chunks, mids, 2, 2 * part, num_rhs), vm(chunks, mids, 2 * part, num_rhs),
+            vm(chunks, 2, mids, 2 * part, num_rhs), vm(chunks, mids, 2 * part, num_rhs),
             vm(mids, max(tops, 8), LANES, dtype=F32), vm(mids, max(tops, 8), LANES, dtype=F32),
             vm(chunks, 2, ny, nx, part, LANES),
             vm(chunks, nx - 1, ny, part, LANES), vm(chunks, ny - 1, nx, part, LANES),
             vm(chunks, ny, part, LANES), vm(chunks, nx, part, LANES),
             vm(chunks, ny - 1, part, LANES), vm(chunks, nx - 1, part, LANES),
             vm(2, chunks, 2 * part, LANES), vm(nx, slab, top_w), vm(nx, slab, LANES),
-            vm(nx, slab, LANES), vm(nx, slab, LANES), vm(per_y, slab, num_rhs),
+            vm(nx, slab, LANES), vm(nx, slab, LANES),
             vm(ny, group, half_rows), vm(ny, nx, group, half_rows),
             vm(tops, 2, rows, half_rows),
             vm(2, nx, nz, wide, rows), vm(nx, nz, wide, rows), vm(nx, nz, wide, rows),
             vm(nz - 1, nx, wide, rows), vm(nx, wide, rows), vm(nx - 1, wide, rows),
             vm(ny, chunk, rows, dtype=F32), vm(ny - 1, chunk, rows, dtype=F32),
-            vm(2, nz, chunk, rows, dtype=F32), vm(chunk, rows, dtype=F32),
-            sems((7,)), sems((10,)), sems((4,)),
-            sems((3 + chunks * (mids + 1),)), sems((3 + chunks * (mids + 1),)),
+            vm(2, nz, chunk, rows, dtype=F32),
+            sems((7,)), sems((10,)),
+            sems((3 + 2 * chunks,)), sems((3 + 2 * chunks,)),
             sems((2, nx)), sems((2, nx)),
             sems((chunks, nx - 1)), sems((chunks, nx - 1)),
             sems((chunks, ny - 1)), sems((chunks, ny - 1)),
@@ -600,13 +587,12 @@
     leaf_x, mid_x, top_solution, outer_part = pl.pallas_call(
         finish_kernel,
         out_shape=tuple(shapes),
-        in_specs=[hbm] * 4,
+        in_specs=[vmem] * 4,
         out_specs=(hbm,) * 4,
-        scratch_shapes=[vm(*a.shape, dtype=a.dtype) for a in results]
-        + [vm(chunk, rows, dtype=F32), sems((4,)), sems((4,))],
+        scratch_shapes=[vm(chunk, rows, dtype=F32), sems((4,))],
         compiler_params=pltpu.CompilerParams(vmem_limit_bytes=60 << 20),
         name="finish",
-    )(*results)
+    )(*[pltpu.with_memory_space_constraint(a, pltpu.VMEM) for a in results])
     return leaf_x, mid_x, top_solution, outer_part.T
 
 

time: 43.1 us -> 41.3 us (0.958)
  Pallas kernels: 42.3 us -> 40.5 us
    pallas_call x2, Pallas kernels: 42.3 us -> 40.5 us  [the longest x1 39.5 us: on_device(): pl.pallas_call(functools.partial(window_kernel, nz, nx, ny), out_shape=(p...]
where the time goes in v4:
time: 41.3 us; the launch traced here: 41.2 us
  Pallas kernels  40.5 us (98%)
  between operations  0.65 us (2%)
    pallas_call x1, Pallas kernels, on_device(): pl.pallas_call(functools.partial(window_kernel, nz, nx, ny), out_shape=(p...  39.5 us
    pallas_call x1, Pallas kernels, on_device(): pl.pallas_call(finish_kernel, out_shape=tuple(shapes), in_specs=[vmem] *...  1.01 us

profile of v4, /device:TPU:1, one launch (start us, length us, event | category | flops | bytes accessed | tf_op | source)
XLA Modules:
  0.0 41.2 jit_solution(3953458202256270526)
XLA Ops:
  0.6 39.5 %window.1 = (bf16[1,8,128,256]{3,2,1,0:T(8,128)(2,1)S(1)}, bf16[1,4,256,256]{3,2,1,0:T(8,128)(2,1)S(1)}, bf16[2,64,256]{2,1,0:T(8,128)(2,1)S(1)}, f32[16,8,128]{2,1,0:T(8,128)S(1)}) custom-call(s32[1,8]{1,0:T(1,128)} %bitcast.7, s32[1,4]{1,0:T(1,128)} %bitcast.8, s32[1,8]{1,0:T(1,128)} %width_leaf_in.1, s32[1,4]{1,0:T(1,128)} %width_mid_in.1, ...), custom_call_target="tpu_custom_call" | custom-call | tf_op jit(solution)/shard_map/window/pallas_call | solution.py:529
  40.1 1.0 %finish.1 = (bf16[1,8,128,256]{3,2,1,0:T(8,128)(2,1)}, bf16[1,4,256,256]{3,2,1,0:T(8,128)(2,1)}, bf16[2,64,256]{2,1,0:T(8,128)(2,1)}, f32[8,128]{1,0:T(8,128)}) custom-call(bf16[1,8,128,256]{3,2,1,0:T(8,128)(2,1)S(1)} %get-tuple-element.12.leaf_x, bf16[1,4,256,256]{3,2,1,0:T(8,128)(2,1)S(1)} %get-tuple-element.13.mid_x, ...), custom_call_target="tpu_custom_call" | custom-call | tf_op jit(solution)/shard_map/finish/pallas_call | solution.py:587

commit v5 on v4

--- a/solution.py
+++ b/solution.py
@@ -314,21 +314,20 @@
                 b2_s.at[q_, d - 1], b2_r.at[q_, d - 1], (z, 2 * tx + c, y),
             ))
             b2_copies[q_][-1].start()
-        if q_ == 0:
-            o_core.wait_recv()
-            oz_copies = []
-
-            def outer_pair(i, carry):
-                o_s[i] = (o_t[c, i].astype(F32) + o_rx[i].astype(F32)).astype(BF16)
-                return carry
-
-            lax.fori_loop(0, nx, outer_pair, 0)
-            for d in range(1, nz):
-                tz = lax.rem(z + d, nz)
-                oz_copies.append(remote(
-                    o_s.at[:, tz], o_rz.at[d - 1], oz_s.at[d - 1], oz_r.at[d - 1], (tz, pc, y),
-                ))
-                oz_copies[-1].start()
+    o_core.wait_recv()
+    oz_copies = []
+
+    def outer_pair(i, carry):
+        o_s[i] = (o_t[c, i].astype(F32) + o_rx[i].astype(F32)).astype(BF16)
+        return carry
+
+    lax.fori_loop(0, nx, outer_pair, 0)
+    for d in range(1, nz):
+        tz = lax.rem(z + d, nz)
+        oz_copies.append(remote(
+            o_s.at[:, tz], o_rz.at[d - 1], oz_s.at[d - 1], oz_r.at[d - 1], (tz, pc, y),
+        ))
+        oz_copies[-1].start()
 
     for i in range(nx):
         pre = [

time: 41.3 us -> 41.1 us (level)
  no operation moved by 1% of the time
where the time goes in v5:
time: 41.1 us; the launch traced here: 41 us
  Pallas kernels  40.3 us (98%)
  between operations  0.65 us (2%)
    pallas_call x1, Pallas kernels, on_device(): pl.pallas_call(functools.partial(window_kernel, nz, nx, ny), out_shape=(p...  39.3 us
    pallas_call x1, Pallas kernels, on_device(): pl.pallas_call(finish_kernel, out_shape=tuple(shapes), in_specs=[vmem] *...  1.01 us

profile of v5, /device:TPU:1, one launch (start us, length us, event | category | flops | bytes accessed | tf_op | source)
XLA Modules:
  0.0 41.0 jit_solution(168094250242618125)
XLA Ops:
  0.6 39.3 %window.1 = (bf16[1,8,128,256]{3,2,1,0:T(8,128)(2,1)S(1)}, bf16[1,4,256,256]{3,2,1,0:T(8,128)(2,1)S(1)}, bf16[2,64,256]{2,1,0:T(8,128)(2,1)S(1)}, f32[16,8,128]{2,1,0:T(8,128)S(1)}) custom-call(s32[1,8]{1,0:T(1,128)} %bitcast.7, s32[1,4]{1,0:T(1,128)} %bitcast.8, s32[1,8]{1,0:T(1,128)} %width_leaf_in.1, s32[1,4]{1,0:T(1,128)} %width_mid_in.1, ...), custom_call_target="tpu_custom_call" | custom-call | tf_op jit(solution)/shard_map/window/pallas_call | solution.py:528
  39.9 1.0 %finish.1 = (bf16[1,8,128,256]{3,2,1,0:T(8,128)(2,1)}, bf16[1,4,256,256]{3,2,1,0:T(8,128)(2,1)}, bf16[2,64,256]{2,1,0:T(8,128)(2,1)}, f32[8,128]{1,0:T(8,128)}) custom-call(bf16[1,8,128,256]{3,2,1,0:T(8,128)(2,1)S(1)} %get-tuple-element.12.leaf_x, bf16[1,4,256,256]{3,2,1,0:T(8,128)(2,1)S(1)} %get-tuple-element.13.mid_x, ...), custom_call_target="tpu_custom_call" | custom-call | tf_op jit(solution)/shard_map/finish/pallas_call | solution.py:586
